TPU v7x, 256 devices: a whole 4x4x8 slice. The times are simulated.
256 devices in a mesh: row: 4 (over y), col: 8 (over z), layer: 8 (over x, core).
Axes of the slice: x: 4, y: 4, z: 8, core: 2. Of those that a mesh axis runs over, the one named last changes fastest.
Arguments:
- left_blocks: bfloat16 [32, 512, 128, 128], P(('row', 'col'), 'layer'), may hold values from -6 to 6
- left_slots: int32 [32, 512], P(('row', 'col'), 'layer'), may hold values from 0 to 255, as said below
- right_blocks: bfloat16 [8, 128, 128, 128], P('layer', ('row', 'col')), may hold values from -6 to 6
- right_slots: int32 [8, 128], P('layer', ('row', 'col')), may hold values from 0 to 255, as said below
- out_slots: int32 [32, 32], P(('row', 'col')), may hold values from 0 to 63, as said below
Outputs:
- inflated: float32 [32, 32, 128, 128], P(('row', 'col'), 'layer')
Inputs may be any that keep to these rules, and one draw needn't show every extreme that they name: `left_slots`: the 64 slots of one device differ from one another. `right_slots`: the slots of one layer differ from one another. `out_slots`: entry o of a row is r * 8 + o % 8; in each block column of the slab a row names 4 different block rows r.
All inputs are finite; a program needn't handle non-finite values.
Results may differ from a plain program's by a relative error of at most 0.0003.
Values may be sent and summed in bfloat16 or wider, within the bound.
A program may use at most 256 MiB of HBM per device.

v0:
```python
import jax
import jax.numpy as jnp
from jax import lax
from jax.sharding import PartitionSpec as P

RB_DEV = 8
KL = 32
SLAB_COLUMNS = 8


def dense_grid(block_set, block_slots, major_count, minor_count):
    block_side = block_set.shape[-1]
    placing = (
        jnp.arange(major_count * minor_count, dtype=jnp.int32)[:, None] == block_slots[None, :]
    ).astype(block_set.dtype)
    block_grid = jnp.einsum(
        "sn,nab->sab", placing, block_set, preferred_element_type=jnp.float32
    ).astype(block_set.dtype)
    block_grid = block_grid.reshape(major_count, minor_count, block_side, block_side).transpose(
        0, 2, 1, 3
    )
    return block_grid.reshape(major_count * block_side, minor_count * block_side)


def select_blocks(product, sparsity_pattern, row_count, number_of_slabs):
    block_side = product.shape[0] // row_count
    block_grid = product.reshape(row_count, block_side, number_of_slabs, block_side)
    return block_grid[sparsity_pattern // number_of_slabs, :, sparsity_pattern % number_of_slabs, :]


def column_totals(expanded_matrix, sparsity_pattern, number_of_slabs):
    row_sums = jnp.sum(expanded_matrix, axis=1)
    onehot = (
        sparsity_pattern[:, None] % number_of_slabs == jnp.arange(number_of_slabs)[None, :]
    ).astype(jnp.float32)
    return jnp.einsum("ns,nc->sc", onehot, row_sums, precision=lax.Precision.HIGHEST)


def apply_inflation(expanded_matrix, sparsity_pattern, number_of_slabs, column_mean):
    onehot = (
        sparsity_pattern[:, None] % number_of_slabs == jnp.arange(number_of_slabs)[None, :]
    ).astype(jnp.float32)
    spread = jnp.einsum("ns,sc->nc", onehot, column_mean, precision=lax.Precision.HIGHEST)
    return expanded_matrix / (spread[:, None, :] + 1e-06)


def body(left_blocks, left_slots, right_blocks, right_slots, out_slots):
    block_side = left_blocks.shape[-1]
    left_grid = dense_grid(left_blocks[0], left_slots[0], RB_DEV, KL)
    gathered_tiles, gathered_places = (
        lax.all_gather(right_blocks[0], ("row", "col"), axis=0, tiled=True),
        lax.all_gather(right_slots[0], ("row", "col"), axis=0, tiled=True),
    )
    right_grid = dense_grid(gathered_tiles, gathered_places, KL, SLAB_COLUMNS)
    product = jnp.dot(left_grid, right_grid, preferred_element_type=jnp.float32)
    sparsity_pattern = out_slots[0]
    partial_value = select_blocks(product, sparsity_pattern, RB_DEV, SLAB_COLUMNS)
    overall_rows = (
        lax.axis_size("row")
        * lax.axis_size("col")
        * (sparsity_pattern.shape[0] // SLAB_COLUMNS)
        * block_side
    )
    owned_count = sparsity_pattern.shape[0] // lax.axis_size("layer")
    owned_slot_list = lax.dynamic_slice_in_dim(
        sparsity_pattern, lax.axis_index("layer") * owned_count, owned_count, 0
    )
    owned_blocks = lax.psum_scatter(partial_value, "layer", scatter_dimension=0, tiled=True)
    expanded_matrix = owned_blocks * owned_blocks
    column_sum_vector = lax.psum(
        column_totals(expanded_matrix, owned_slot_list, SLAB_COLUMNS), ("row", "col", "layer")
    )
    slab_output = apply_inflation(
        expanded_matrix, owned_slot_list, SLAB_COLUMNS, column_sum_vector / overall_rows
    )
    return slab_output[None]


def solution(mesh):
    return jax.shard_map(
        body,
        mesh=mesh,
        in_specs=(
            P(("row", "col"), "layer", None, None),
            P(("row", "col"), "layer"),
            P("layer", ("row", "col"), None, None),
            P("layer", ("row", "col")),
            P(("row", "col"), None),
        ),
        out_specs=P(("row", "col"), "layer", None, None),
        check_vma=False,
    )
```

profile of v0, /device:TPU:2, one launch (start us, length us, event | category | flops | bytes accessed | tf_op | source)
XLA Modules:
  0.0 280.0 jit_solution(13103965245307222590)
XLA Ops:
  6.5 0.0 copy-start
  6.5 0.0 all-gather.4.cloned.1.call-start
  6.5 0.7 all-gather.4.cloned.1.call-update
  7.3 0.0 reduce-scatter.2.cloned.1.call-start
  7.3 0.8 copy-done
  8.1 6.4 %convolution_convert_fusion = bf16[256,128,128]{2,0,1:T(8,128)(2,1)} fusion(bf16[64,128,128]{2,1,0:T(8,128)(2,1)S(1)} %bitcast.60, s32[64]{0:T(128)} %bitcast.67), kind=kOutput, calls=%fused_computation.5 | convolution fusion | flops 541081600 | bytes 10486016 | tf_op jit(solution)/shard_map/sn,nab->sab/dot_general | solution.py:16
  14.6 0.0 copy-start.3
  14.6 0.0 copy-start.1
  14.6 0.0 copy-start.2
  14.6 13.4 %reshape.188 = bf16[8,128,4096]{2,0,1:T(8,128)(2,1)} reshape(bf16[8,128,32,128]{3,2,0,1:T(8,128)(2,1)} %bitcast.63) | data formatting | bytes 16777216 | tf_op jit(solution)/shard_map/dot_general | solution.py:55
  28.0 0.0 copy-done.3
  28.0 0.6 dynamic-slice.1
  29.2 0.0 copy-done.1
  29.2 0.1 bitcast_dynamic-update-slice_fusion
  29.3 23.9 %all-reduce = s32[128]{0:T(128)S(1)} all-reduce(s32[128]{0:T(128)S(1)} %bitcast_dynamic-update-slice_fusion), channel_id=2, replica_groups=mesh['row'=4,'col'=8,'layer'=8] {'row','col'}, use_global_device_ids=true, to_apply=%add | all-reduce | flops 128 | bytes 1024
  53.2 0.0 copy-done.2
  53.2 41.5 %all-gather.4.cloned.1.call-done = bf16[1,128,128,128]{3,2,0,1:T(8,128)(2,1)} async-done(((bf16[1,4,128,128]{3,2,0,1:T(8,128)(2,1)}), bf16[1,128,128,128]{3,2,0,1:T(8,128)(2,1)}) %all-gather.4.cloned.1.call-update) | async-done | bytes 4194320 | tf_op jit(solution)/shard_map/all_gather | solution.py:51
  94.7 9.5 %convert_bitcast_fusion = bf16[32,8,128,128]{3,1,0,2:T(8,128)(2,1)} fusion(bf16[1,128,128,128]{3,2,0,1:T(8,128)(2,1)} %all-gather.4.cloned.1.call-done, s32[128]{0:T(128)S(1)} %all-reduce), kind=kOutput, calls=%fused_computation.4 | convolution fusion | flops 1077968896 | bytes 12583424 | tf_op jit(solution)/shard_map/sn,nab->sab/dot_general | solution.py:16
  104.2 8.9 %copy.18 = bf16[32,8,128,128]{3,1,2,0:T(8,128)(2,1)} copy(bf16[32,8,128,128]{3,1,0,2:T(8,128)(2,1)} %convert_bitcast_fusion) | data formatting | bytes 16777216 | tf_op jit(solution)/shard_map/reshape | solution.py:19
  113.2 8.8 %copy.35 = bf16[512,8,8,128]{3,1,2,0:T(8,128)(2,1)} copy(bf16[512,8,8,128]{3,2,1,0:T(8,128)(2,1)} %bitcast.61) | data formatting | bytes 16777216
  121.9 11.5 %copy.24 = bf16[1024,4096]{1,0:T(8,128)(2,1)} copy(bf16[1024,4096]{0,1:T(8,128)(2,1)} %bitcast.62) | data formatting | bytes 16777216 | tf_op jit(solution)/shard_map/dot_general | solution.py:55
  133.4 24.7 %fusion = f32[8,128,8,128]{3,1,2,0:T(8,128)} fusion(bf16[8,128,4096,1]{2,1,0,3:T(8,128)(2,1)} %bitcast.65, bf16[8,128,4096,1]{2,0,1,3:T(8,128)(2,1)} %bitcast.64), kind=kOutput, calls=%fused_computation.2 | convolution fusion | flops 8589934592 | bytes 20971520 | tf_op jit(solution)/shard_map/dot_general | solution.py:55
  158.1 4.2 %gather_fusion = f32[32,128,128]{2,1,0:T(8,128)} fusion(f32[8,128,8,128]{3,1,2,0:T(8,128)} %fusion, s32[32]{0:T(128)S(1)} %fusion.22), kind=kCustom, calls=%fused_computation | custom fusion | bytes 4194560 | tf_op jit(solution)/shard_map/gather | solution.py:28
  162.3 0.0 reduce-scatter.2.cloned.1.call-update
  162.4 0.1 and_select_fusion
  162.4 30.2 %reduce-scatter.2.cloned.1.call-done = f32[4,128,128]{2,1,0:T(8,128)} async-done(((f32[32,128,128]{2,1,0:T(8,128)}), f32[4,128,128]{2,1,0:T(8,128)}) %reduce-scatter.2.cloned.1.call-update) | async-done | bytes 262160 | tf_op jit(solution)/shard_map/reduce_scatter | solution.py:68
  192.7 1.0 multiply_reduce_fusion
  193.6 0.3 fusion.13
  193.9 77.4 %psum.7 = f32[8,128]{1,0:T(8,128)S(1)} all-reduce(f32[8,128]{1,0:T(8,128)S(1)} %fusion.13), channel_id=1, replica_groups=mesh['row'=4,'col'=8,'layer'=8] {'row','col','layer'}, use_global_device_ids=true, to_apply=%region_2.3 | all-reduce | flops 1024 | bytes 8192 | tf_op jit(solution)/shard_map/psum | solution.py:70
  271.3 0.2 convolution_add_fusion
  271.5 1.7 divide_bitcast_fusion
  (2 shorter events, 0.0 us)
Async XLA Ops:
  6.5 1.6 copy-start
  6.5 88.2 %all-gather.4.cloned.1.call-start = ((), (), s32[]{:S(2)}) async-start(), calls=%async_computation.2 | async-start | bytes 4325376 | tf_op jit(solution)/shard_map/all_gather | solution.py:51
  7.3 185.4 %reduce-scatter.2.cloned.1.call-start = ((), (), s32[]{:S(2)}) async-start(), calls=%async_computation.1 | async-start | bytes 2359296 | tf_op jit(solution)/shard_map/reduce_scatter | solution.py:68
  14.6 13.4 %copy-start.3 = (u32[256]{0:T(256)S(1)}, u32[256]{0:T(256)}, u32[]{:S(2)}) copy-start(u32[256]{0:T(256)} %constant.78) | copy-start | bytes 3076
  14.6 14.7 %copy-start.1 = (s32[1,4]{1,0:T(1,128)S(1)}, s32[1,4]{1,0:T(1,128)}, u32[]{:S(2)}) copy-start(s32[1,4]{1,0:T(1,128)} %param.8) | copy-start | bytes 52
  14.6 38.6 %copy-start.2 = (s32[1,32]{1,0:T(1,128)S(1)}, s32[1,32]{1,0:T(1,128)}, u32[]{:S(2)}) copy-start(s32[1,32]{1,0:T(1,128)} %param.9) | copy-start | bytes 388
Sparse Core Ops, SparseCore 0:
  10.0 84.7 all-gather.3
  162.5 30.1 reduce-scatter.1
where the time goes:
time: 284 us; the launch traced here: 280 us
  blocking collectives  101 us (36%)
  waiting for transfers between devices  72.4 us (25%)
  local copies, waits for them, and re-layouts  48.3 us (17%)
  matrix products  41.1 us (14%)
  between operations  14.1 us (5%)
    psum x1, blocking collectives, body(): lax.psum(column_totals(expanded_matrix, owned_slot_list, SLAB_COLUMNS), (...  77.4 us
    all_gather x1, waiting for transfers between devices, body(): lax.all_gather(right_blocks[0], ('row', 'col'), axis=0, tiled=True)  41.5 us
    reduce_scatter x1, waiting for transfers between devices, body(): lax.psum_scatter(partial_value, 'layer', scatter_dimension=0, tiled=True)  30.2 us
    dot_general x2, local copies, waits for them, and re-layouts, body(): product = jnp.dot(left_grid, right_grid, preferred_element_type=jnp.float32)  24.9 us
    dot_general x1, matrix products, body(): product = jnp.dot(left_grid, right_grid, preferred_element_type=jnp.float32)  24.7 us
    unnamed x1, blocking collectives  23.9 us
    dot_general x2, matrix products, dense_grid(): jnp.einsum('sn,nab->sab', placing, block_set, preferred_element_type=jnp....  15.9 us
    unnamed x12, local copies, waits for them, and re-layouts  10.3 us
  transfers between devices with their start and end apart: 2, of which 2 were waited for; matrix products, arithmetic and copies ran while one was open for 7% of the time, Pallas kernels for 0%

commit v1 on v0

v1 whole, which is shorter than its diff:
```python
import jax
import jax.numpy as jnp
from jax import lax
from jax.experimental import pallas as pl
from jax.experimental.pallas import tpu as pltpu
from jax.sharding import PartitionSpec as P

MESH = pl.DeviceIdType.MESH
F32 = jnp.float32
BF16 = jnp.bfloat16
I32 = jnp.int32

BS = 128
NY, NZ, NX = 4, 8, 4
ROWS = 4 * BS
A_ROWS, B_ROWS = 304, 208
A_CUT, B_CUT = 160, 96
Z_INDEX = {0: 0, 1: 1, -1: 2, 2: 3, -2: 4, 3: 5, -3: 6, 4: 7}
Y_INDEX = {0: 0, 1: 1, -1: 2, 2: 3}
SOURCES = (
    (0, 0), (0, 1), (0, 2), (1, 0), (2, 0), (1, 1), (1, 2), (2, 1), (2, 2), (3, 0), (0, 3), (0, 4),
    (3, 1), (3, 2), (1, 3), (2, 3), (1, 4), (2, 4), (0, 6), (1, 5), (2, 5), (1, 6), (2, 6), (3, 3),
    (3, 4), (0, 5), (3, 5), (3, 6), (1, 7), (2, 7), (3, 7), (0, 7),
)
GROUPS = (4, 6, 8, 2, 4, 4, 4)
PROGRAM = (
    0, 200, 4, 6, 14, 10, 12, 32, 36, -5, 5, -1, -7, -15, 1, 7, 16, 18, -11, -13, -33, -37, 201,
    202, 203, 204, 11, 13, 40, 44, 15, 37, 400, -6, 300, -2, -8, 2, 8, 20, 22, 33, 300, -17, -19,
    17, 19, -41, -45, 205, 206, 207, 208, -12, 48, 52, 45, -14, -16, 209, 300, -38, 210, -3, 3, 41,
    300, 300, -34, 211, -9, 9, 24, 26, -21, 21, -49, -53, 49, 53, 34, -23, -4, -18, -20, 212, 213,
    -46, 214, 215, 46, -10, 28, 30, 23, -42, 216, 217, 42, 300, -54, 54, 38, -50, 50, 300, -25, 25,
    -27, 27, -35, 218, 35, 300, 300, -22, -47, 219, 220, 47, -31, 31, 300, -55, 55, -43, 221, 222,
    43, -29, 29, -24, 223, 224, 300, -39, 225, 39, -51, 51, -36, 300, -26, -28, 226, 227, -48, -44,
    228, 229, -56, -32, -30, 300, -52, 230, -40, 231, 300, 300, 300,
)
STEP = 8
NG = len(GROUPS)
NONE = 128


def wrap(value, count):
    value = value % count
    return value - count if value > count // 2 else value


def gather_copies():
    copies = []

    def part(kind, sign, whole):
        size, cut = (A_ROWS, A_CUT) if kind == 0 else (B_ROWS, B_CUT)
        if whole:
            return 0, size
        return (0, cut) if sign == 1 else (cut, size - cut)

    for sign in (1, -1):
        for d in range(1, 5):
            src = ((0, 1), (Z_INDEX[-sign * (d - 1)], 1))
            dst = ((0, 1), (Z_INDEX[wrap(-sign * d, NZ)], 1))
            copies.append((0, 1, sign, src, dst) + part(0, sign, d < 4) + (d == 1,))
        for d in (1, 2):
            src = ((0, 1), (Y_INDEX[-sign * (d - 1)], 1))
            dst = ((0, 1), (Y_INDEX[wrap(-sign * d, NY)], 1))
            copies.append((1, 0, sign, src, dst) + part(1, sign, d < 2) + (d == 1,))
    for first, count in ((0, 1), (1, 2), (3, 2), (5, 2), (7, 1)):
        for sign in (1, -1):
            for d in (1, 2):
                src = ((Y_INDEX[-sign * (d - 1)], 1), (first, count))
                dst = ((Y_INDEX[wrap(-sign * d, NY)], 1), (first, count))
                own = first == 0 and d == 1
                copies.append((0, 0, sign, src, dst) + part(0, sign, d < 2) + (own,))
    for first, count in ((0, 1), (1, 2), (3, 1)):
        for sign in (1, -1):
            for d in range(1, 5):
                src = ((Z_INDEX[-sign * (d - 1)], 1), (first, count))
                dst = ((Z_INDEX[wrap(-sign * d, NZ)], 1), (first, count))
                own = first == 0 and d == 1
                copies.append((1, 1, sign, src, dst) + part(1, sign, d < 4) + (own,))
    return copies


COPIES = gather_copies()
N_SMALL = 7 + 3
N_X = 4 * 6
N_SUM = 15 + 7
SEND_SMALL = len(COPIES)
SEND_SIB = SEND_SMALL + N_SMALL
SEND_X = SEND_SIB + 4
SEND_SUM = SEND_X + N_X
N_SEM = SEND_SUM + N_SUM


def to_column(row, eye):
    return jnp.sum(jnp.where(eye, jnp.broadcast_to(row, (BS, BS)), 0), axis=1, keepdims=True)


def kernel(
    left_slots, right_slots, out_slots, left, right, squares, sums,
    left_set, gather_a, gather_b, stage, products, slots_row, slots, meta, meta_s,
    left_s, right_s, out_s, sib_send, sib_recv, partial, half_recv, full_recv,
    sums_xy, sums_z, squared, send_sem, recv_sem, local_sem,
):
    y, z, layer = lax.axis_index("row"), lax.axis_index("col"), lax.axis_index("layer")
    x, core = layer // 2, lax.rem(layer, 2)

    def along_y(d):
        return (lax.rem(y + (d % NY), NY), z, layer)

    def along_z(d):
        return (y, lax.rem(z + (d % NZ), NZ), layer)

    def along_xy(dx, dy):
        return (lax.rem(y + dy % NY, NY), z, lax.rem(x + dx % NX, NX) * 2 + core)

    sibling = (y, z, x * 2 + (1 - core))
    xy_peers = [(dx, dy) for dx in range(NX) for dy in range(NY) if dx or dy]

    local = [
        pltpu.make_async_copy(right_slots, right_s, local_sem.at[0]),
        pltpu.make_async_copy(left_slots, left_s, local_sem.at[1]),
        pltpu.make_async_copy(out_slots, out_s, local_sem.at[2]),
        pltpu.make_async_copy(left, left_set.at[pl.ds(0, 64)], local_sem.at[3]),
    ] + [
        pltpu.make_async_copy(right.at[pl.ds(q * BS, BS)], stage.at[q], local_sem.at[4 + q])
        for q in range(4)
    ]
    for copy in local:
        copy.start()

    barrier = pltpu.get_barrier_semaphore()
    peers = [along_z(d) for d in range(1, NZ)] + [along_xy(*p) for p in xy_peers] + [sibling]
    for peer in peers:
        pl.semaphore_signal(barrier, 1, device_id=peer, device_id_type=MESH)
    pl.semaphore_wait(barrier, len(peers))

    def remote(number, src, dst, device):
        return pltpu.make_async_remote_copy(
            src_ref=src, dst_ref=dst, send_sem=send_sem.at[number], recv_sem=recv_sem.at[number],
            device_id=device, device_id_type=MESH,
        )

    def gather_copy(n):
        kind, axis, sign, src, dst, row, rows, own = COPIES[n]
        buffer = gather_a if kind == 0 else gather_b

        def place(where):
            (p, _), (q, qn) = where
            if qn == 1:
                return buffer.at[p, q, pl.ds(row, rows)]
            return buffer.at[p, pl.ds(q, qn), pl.ds(row, rows)]

        source = right.at[pl.ds((0 if kind == 0 else A_ROWS) + row, rows)] if own else place(src)
        return remote(n, source, place(dst), along_z(sign) if axis else along_y(sign))

    def small_copy(n):
        if n < 7:
            d = n + 1
            return remote(
                SEND_SMALL + n, slots.at[0, 0], slots.at[0, Z_INDEX[wrap(-d, NZ)]], along_z(d)
            )
        d = n - 6
        return remote(SEND_SMALL + n, slots.at[0], slots.at[Y_INDEX[wrap(-d, NY)]], along_y(d))

    lane = lax.broadcasted_iota(I32, (1, BS), 1)

    def send_slots():
        local[0].wait()
        row = jnp.zeros((1, BS), I32)
        for q in range(4):
            row = jnp.where((lane & 3) == q, right_s[0, q], row)
        slots[0, 0] = row
        for n in range(7):
            small_copy(n).start()

    def forward_slots():
        for n in range(7):
            small_copy(n).wait_recv()
        for n in range(7, N_SMALL):
            small_copy(n).start()

    def sort_slots():
        for n in range(7, N_SMALL):
            small_copy(n).wait_recv()
        row_id = lax.broadcasted_iota(I32, (BS, BS), 0)
        lane_id = lax.broadcasted_iota(I32, (BS, BS), 1)
        eye = row_id == lane_id
        slot = jnp.zeros((1, BS), I32)
        for p, (yi, zi) in enumerate(SOURCES):
            slot = jnp.where((lane >> 2) == p, slots[yi, zi], slot)
        group = jnp.zeros((1, BS), I32)
        first = 0
        for size in GROUPS[:-1]:
            first += size
            group = group + ((lane >> 2) >= first).astype(I32)
        segment = group * 8 + (slot & 7)
        key = segment * BS + lane
        key_column = to_column(key, eye)
        rank = jnp.sum((key_column < key).astype(I32), axis=0, keepdims=True)
        segment_column = key_column >> 7
        before = jnp.sum((segment_column < segment).astype(I32), axis=0, keepdims=True)
        opens = (before == rank).astype(I32)
        packed = (rank << 16) | (opens << 15) | (slot << 7) | lane
        packed_column = to_column(packed, eye)
        here = (packed_column >> 16) == lane_id
        meta[0:1, :] = jnp.sum(jnp.where(here, packed_column & 0xFFFF, 0), axis=0, keepdims=True)
        upto = jnp.sum((segment_column <= lane_id).astype(I32), axis=0, keepdims=True)
        count = jnp.sum((segment_column == lane_id).astype(I32), axis=0, keepdims=True)
        meta[1:2, :] = jnp.where(count > 0, upto - 1, NONE)
        local[1].wait()
        inverse = [jnp.full((1, BS), 64, I32), jnp.full((1, BS), 64, I32)]
        for n in range(64):
            place = left_s[0, n]
            for h in range(2):
                inverse[h] = jnp.where(lane + h * BS == place, n, inverse[h])
        meta[2:3, :] = inverse[0]
        meta[3:4, :] = inverse[1]
        copy = pltpu.make_async_copy(meta, meta_s, local_sem.at[8])
        copy.start()
        copy.wait()
        for copy in local[2:]:
            copy.wait()

    def stage_source(p):
        if p == 0:
            return
        yi, zi = SOURCES[p]
        a_tail = A_ROWS - 2 * BS
        b_head = BS - a_tail
        stage[4 * p] = gather_a[yi, zi, pl.ds(0, BS)]
        stage[4 * p + 1] = gather_a[yi, zi, pl.ds(BS, BS)]
        stage[4 * p + 2, pl.ds(0, a_tail)] = gather_a[yi, zi, pl.ds(2 * BS, a_tail)]
        stage[4 * p + 2, pl.ds(a_tail, b_head)] = gather_b[zi, yi, pl.ds(0, b_head)]
        stage[4 * p + 3] = gather_b[zi, yi, pl.ds(b_head, BS)]

    def multiply(start):
        for t in range(start, start + STEP):
            word = meta_s[0, t]
            block, slot, opens = word & 127, (word >> 7) & 255, word >> 15
            k, j = slot >> 3, slot & 7
            chosen = []
            for m in range(4):
                r = out_s[0, lax.rem(x + m, NX) * 8 + j] >> 3
                at = r * 32 + k
                chosen.append(left_set[meta_s[2 + (at >> 7), at & 127]])
            product = jnp.dot(
                jnp.concatenate(chosen, axis=0), stage[block], preferred_element_type=F32
            )
            previous = opens * NONE + (1 - opens) * (t - 1)
            products[t] = product + products[previous]

    left_set[64] = jnp.zeros((BS, BS), BF16)
    products[NONE] = jnp.zeros((ROWS, BS), F32)

    done = 0
    opened = 0
    for item in PROGRAM:
        if item < 0:
            gather_copy(-1 - item).wait_recv()
        elif item < 200:
            gather_copy(item).start()
            opened += 1
            if opened == 8:
                send_slots()
        elif item < 300:
            if item == 201:
                forward_slots()
            stage_source(item - 200)
        elif item == 300:
            multiply(done)
            done += STEP
        else:
            sort_slots()

    def column_sum(j):
        total = products[meta_s[1, j]]
        for g in range(1, NG):
            total = total + products[meta_s[1, g * 8 + j]]
        return total

    def sib_copy(jj):
        return remote(SEND_SIB + jj, sib_send.at[jj], sib_recv.at[jj], sibling)

    for jj in range(4):
        sib_send[jj] = column_sum((1 - core) * 4 + jj)
        sib_copy(jj).start()
    for jj in range(4):
        partial[jj] = column_sum(core * 4 + jj)

    half = BS // 2

    def x_copy(jj, what):
        number = SEND_X + jj * 6 + what
        forth = what % 2 == 0
        side = 0 if forth else 1
        device = along_xy(1, 0) if forth else along_xy(-1, 0)
        if what < 2:
            src = partial.at[jj, pl.ds(2 * BS + side * half, half)]
            dst = half_recv.at[side, jj]
        else:
            base = BS if forth else 3 * BS
            row = (half if forth else 0) if what < 4 else (0 if forth else half)
            src = partial.at[jj, pl.ds(base + row, half)]
            dst = full_recv.at[side, jj, pl.ds(row, half)]
        return remote(number, src, dst, device)

    for jj in range(4):
        sib_copy(jj).wait_recv()
        partial[jj] = partial[jj] + sib_recv[jj]
        x_copy(jj, 0).start()
        x_copy(jj, 1).start()
    for jj in range(4):
        x_copy(jj, 2).start()
        x_copy(jj, 3).start()
    for jj in range(4):
        x_copy(jj, 0).wait_recv()
        partial[jj, pl.ds(BS, half)] = partial[jj, pl.ds(BS, half)] + half_recv[0, jj]
        x_copy(jj, 4).start()
        x_copy(jj, 1).wait_recv()
        partial[jj, pl.ds(3 * BS + half, half)] = (
            partial[jj, pl.ds(3 * BS + half, half)] + half_recv[1, jj]
        )
        x_copy(jj, 5).start()
    stores = []
    for jj in range(4):
        for what in (2, 3, 4, 5):
            x_copy(jj, what).wait_recv()
        total = partial[jj, pl.ds(0, BS)] + full_recv[0, jj] + full_recv[1, jj]
        square = total * total
        squared[jj] = square
        stores.append(pltpu.make_async_copy(squared.at[jj], squares.at[jj], local_sem.at[9 + jj]))
        stores[-1].start()
        sums_xy[0, jj : jj + 1, :] = jnp.sum(square, axis=0, keepdims=True)

    def xy_copy(n):
        dx, dy = xy_peers[n]
        slot = ((-dx) % NX) * NY + (-dy) % NY
        return remote(SEND_SUM + n, sums_xy.at[0], sums_xy.at[slot], along_xy(dx, dy))

    def z_copy(n):
        d = n + 1
        return remote(SEND_SUM + 15 + n, sums_z.at[0], sums_z.at[(-d) % NZ], along_z(d))

    for n in range(15):
        xy_copy(n).start()
    total = sums_xy[0]
    for n in range(15):
        xy_copy(n).wait_recv()
    for n in range(1, 16):
        total = total + sums_xy[n]
    sums_z[0] = total
    for n in range(7):
        z_copy(n).start()
    for n in range(7):
        z_copy(n).wait_recv()
    for n in range(1, NZ):
        total = total + sums_z[n]
    meta_sum = sums_xy.at[1]
    meta_sum[...] = total
    last = pltpu.make_async_copy(meta_sum, sums, local_sem.at[13])
    last.start()

    for n in range(len(COPIES)):
        gather_copy(n).wait_send()
    for n in range(N_SMALL):
        small_copy(n).wait_send()
    for jj in range(4):
        sib_copy(jj).wait_send()
        for what in range(6):
            x_copy(jj, what).wait_send()
        stores[jj].wait()
    for n in range(15):
        xy_copy(n).wait_send()
    for n in range(7):
        z_copy(n).wait_send()
    last.wait()


def body(left_blocks, left_slots, right_blocks, right_slots, out_slots):
    any_spec = pl.BlockSpec(memory_space=pl.ANY)
    squares, sums = pl.pallas_call(
        kernel,
        out_shape=(
            jax.ShapeDtypeStruct((4, BS, BS), F32),
            jax.ShapeDtypeStruct((4, BS), F32),
        ),
        in_specs=[any_spec] * 5,
        out_specs=(any_spec, any_spec),
        scratch_shapes=[
            pltpu.VMEM((65, BS, BS), BF16),
            pltpu.VMEM((NY, NZ, A_ROWS, BS), BF16),
            pltpu.VMEM((NZ, NY, B_ROWS, BS), BF16),
            pltpu.VMEM((32 * 4, BS, BS), BF16),
            pltpu.VMEM((NONE + 1, ROWS, BS), F32),
            pltpu.VMEM((1, BS), I32),
            pltpu.VMEM((NY, NZ, 1, BS), I32),
            pltpu.VMEM((8, BS), I32),
            pltpu.SMEM((8, BS), I32),
            pltpu.SMEM((1, 64), I32),
            pltpu.SMEM((1, 4), I32),
            pltpu.SMEM((1, 32), I32),
            pltpu.VMEM((4, ROWS, BS), F32),
            pltpu.VMEM((4, ROWS, BS), F32),
            pltpu.VMEM((4, ROWS, BS), F32),
            pltpu.VMEM((2, 4, BS // 2, BS), F32),
            pltpu.VMEM((2, 4, BS, BS), F32),
            pltpu.VMEM((16, 4, BS), F32),
            pltpu.VMEM((NZ, 4, BS), F32),
            pltpu.VMEM((4, BS, BS), F32),
            pltpu.SemaphoreType.DMA((N_SEM,)),
            pltpu.SemaphoreType.DMA((N_SEM,)),
            pltpu.SemaphoreType.DMA((14,)),
        ],
        compiler_params=pltpu.CompilerParams(
            collective_id=0, has_side_effects=True, vmem_limit_bytes=60 * 2**20
        ),
        name="expand_and_sum",
    )(
        left_slots,
        right_slots,
        out_slots,
        left_blocks.reshape(64, BS, BS),
        right_blocks.reshape(ROWS, BS),
    )
    rows = NY * NZ * 4 * BS
    return (squares / (sums[:, None, :] / rows + 1e-6))[None]


def solution(mesh):
    return jax.shard_map(
        body,
        mesh=mesh,
        in_specs=(
            P(("row", "col"), "layer", None, None),
            P(("row", "col"), "layer"),
            P("layer", ("row", "col"), None, None),
            P("layer", ("row", "col")),
            P(("row", "col"), None),
        ),
        out_specs=P(("row", "col"), "layer", None, None),
        check_vma=False,
    )
```

time: 284 us -> 68.3 us (0.24); the launches traced: 280 us -> 67.9 us
  blocking collectives: 101 us -> 0 us
  waiting for transfers between devices: 72.4 us -> 0 us
  Pallas kernels: 0 us -> 65.5 us
  local copies, waits for them, and re-layouts: 48.3 us -> 0 us
  matrix products: 41.1 us -> 0 us
  between operations: 14.1 us -> 0.01 us
    psum x1 -> x0, blocking collectives: 77.4 us -> none  [body(): lax.psum(column_totals(expanded_matrix, owned_slot_list, SLAB_COLUMNS), (...]
    pallas_call x0 -> x1, Pallas kernels: none -> 65.5 us  [body(): pl.pallas_call(kernel, out_shape=(jax.ShapeDtypeStruct((4, BS, BS), F32),...]
    all_gather x1 -> x0, waiting for transfers between devices: 41.5 us -> none  [body(): lax.all_gather(right_blocks[0], ('row', 'col'), axis=0, tiled=True)]
    dot_general x5 -> x0, matrix products: 41.1 us -> none  [the longest x1 24.7 us: body(): product = jnp.dot(left_grid, right_grid, preferred_element_type=jnp.float32)]
    reduce_scatter x1 -> x0, waiting for transfers between devices: 30.2 us -> none  [body(): lax.psum_scatter(partial_value, 'layer', scatter_dimension=0, tiled=True)]
    dot_general x2 -> x0, local copies, waits for them, and re-layouts: 24.9 us -> none  [body(): product = jnp.dot(left_grid, right_grid, preferred_element_type=jnp.float32)]
    unnamed x1 -> x0, blocking collectives: 23.9 us -> none
    unnamed x12 -> x0, local copies, waits for them, and re-layouts: 10.3 us -> none
  transfers between devices with their start and end apart: 2 -> 0, of which waited for: 2 -> 0; matrix products, arithmetic and copies ran while one was open for 7% -> 0% of each run, Pallas kernels for 0% -> 0%
where the time goes in v1:
time: 68.3 us; the launch traced here: 67.9 us
  Pallas kernels  65.5 us (96%)
  other arithmetic  2.35 us (3%)
    pallas_call x1, Pallas kernels, body(): pl.pallas_call(kernel, out_shape=(jax.ShapeDtypeStruct((4, BS, BS), F32),...  65.5 us
    broadcast_in_dim x1, other arithmetic, body(): return (squares / (sums[:, None, :] / rows + 1e-06))[None]  1.68 us

profile of v1, /device:TPU:2, one launch (start us, length us, event | category | flops | bytes accessed | tf_op | source)
XLA Modules:
  0.0 67.9 jit_solution(10990750999978471651)
XLA Ops:
  0.0 65.5 %expand_and_sum.1 = (f32[4,128,128]{2,1,0:T(8,128)}, f32[4,128]{1,0:T(4,128)}) custom-call(s32[1,64]{1,0:T(1,128)} %left_slots.1, s32[1,4]{1,0:T(1,128)} %right_slots.1, s32[1,32]{1,0:T(1,128)} %out_slots.1, bf16[64,128,128]{2,1,0:T(8,128)(2,1)} %bitcast.4, bf16[512,128]{1,0:T(8,128)(2,1)} %bitcast.5), custom_call_target="tpu_custom_call" | custom-call | tf_op jit(solution)/shard_map/expand_and_sum/pallas_call | solution.py:379
  65.5 0.7 multiply_add_fusion
  66.2 1.7 %divide_bitcast_fusion = f32[1,4,128,128]{3,2,1,0:T(8,128)} fusion(f32[4,128,128]{2,1,0:T(8,128)} %get-tuple-element.7, f32[4,128]{1,0:T(4,128)S(1)} %multiply_add_fusion), kind=kLoop, calls=%fused_computation | loop fusion | flops 65536 | bytes 526336 | tf_op jit(solution)/shard_map/broadcast_in_dim | solution.py:424

commit v2 on v1

--- a/solution.py
+++ b/solution.py
@@ -18,23 +18,24 @@
 Z_INDEX = {0: 0, 1: 1, -1: 2, 2: 3, -2: 4, 3: 5, -3: 6, 4: 7}
 Y_INDEX = {0: 0, 1: 1, -1: 2, 2: 3}
 SOURCES = (
-    (0, 0), (0, 1), (0, 2), (1, 0), (2, 0), (1, 1), (1, 2), (2, 1), (2, 2), (3, 0), (0, 3), (0, 4),
-    (3, 1), (3, 2), (1, 3), (2, 3), (1, 4), (2, 4), (0, 6), (1, 5), (2, 5), (1, 6), (2, 6), (3, 3),
-    (3, 4), (0, 5), (3, 5), (3, 6), (1, 7), (2, 7), (3, 7), (0, 7),
+    (0, 0), (0, 1), (0, 2), (1, 0), (2, 0), (0, 3), (1, 2), (2, 2), (1, 1), (2, 1), (0, 4), (0, 5),
+    (3, 1), (3, 2), (3, 0), (1, 4), (2, 4), (1, 3), (2, 3), (3, 4), (3, 3), (0, 6), (1, 5), (2, 5),
+    (1, 6), (2, 6), (0, 7), (3, 5), (3, 6), (1, 7), (2, 7), (3, 7),
 )
-GROUPS = (4, 6, 8, 2, 4, 4, 4)
+GROUPS = (4, 6, 8, 4, 4, 2, 2, 2)
 PROGRAM = (
-    0, 200, 4, 6, 14, 10, 12, 32, 36, -5, 5, -1, -7, -15, 1, 7, 16, 18, -11, -13, -33, -37, 201,
-    202, 203, 204, 11, 13, 40, 44, 15, 37, 400, -6, 300, -2, -8, 2, 8, 20, 22, 33, 300, -17, -19,
-    17, 19, -41, -45, 205, 206, 207, 208, -12, 48, 52, 45, -14, -16, 209, 300, -38, 210, -3, 3, 41,
-    300, 300, -34, 211, -9, 9, 24, 26, -21, 21, -49, -53, 49, 53, 34, -23, -4, -18, -20, 212, 213,
-    -46, 214, 215, 46, -10, 28, 30, 23, -42, 216, 217, 42, 300, -54, 54, 38, -50, 50, 300, -25, 25,
-    -27, 27, -35, 218, 35, 300, 300, -22, -47, 219, 220, 47, -31, 31, 300, -55, 55, -43, 221, 222,
-    43, -29, 29, -24, 223, 224, 300, -39, 225, 39, -51, 51, -36, 300, -26, -28, 226, 227, -48, -44,
-    228, 229, -56, -32, -30, 300, -52, 230, -40, 231, 300, 300, 300,
+    6, 4, 0, 10, 401, 36, 32, 14, 200, 12, -5, -11, 11, 5, -7, 7, -1, 1, 16, 18, -33, -13, 13, 40,
+    -37, 201, 37, -15, 402, 202, -6, 33, -12, 44, -8, 8, -2, 20, 22, 2, -41, -19, -38, 203, 38, 48,
+    -17, 52, 400, -34, 15, 204, -45, 205, 206, 19, 41, 45, 17, -14, 207, -3, 3, -9, -23, 34, 23,
+    300, -16, -21, 21, 300, 208, -39, 24, 26, 209, 300, -49, 9, -53, 210, 49, -20, 211, -18, 53,
+    300, 212, 300, 213, -42, 214, 215, 42, 216, -4, -24, -22, -46, 46, 217, 39, 300, 218, -10, 28,
+    30, 300, 300, -50, 219, 50, 300, -54, 54, -35, -27, 35, 27, 220, 221, 300, -25, 25, 300, -47,
+    -43, 222, 223, 224, -31, 47, 43, 31, 225, 300, -40, -29, -51, 300, -55, 29, -28, -36, 51, 55,
+    500, 226, -26, 227, 228, 300, -48, -44, -32, 229, 300, -52, -56, 230, -30, 231, 300,
 )
 STEP = 8
 NG = len(GROUPS)
+FOLDED = 5
 NONE = 128
 
 
@@ -113,6 +114,7 @@
 
     sibling = (y, z, x * 2 + (1 - core))
     xy_peers = [(dx, dy) for dx in range(NX) for dy in range(NY) if dx or dy]
+    xy_peers.sort(key=lambda p: -min(p[0], NX - p[0]) - min(p[1], NY - p[1]))
 
     local = [
         pltpu.make_async_copy(right_slots, right_s, local_sem.at[0]),
@@ -127,7 +129,8 @@
         copy.start()
 
     barrier = pltpu.get_barrier_semaphore()
-    peers = [along_z(d) for d in range(1, NZ)] + [along_xy(*p) for p in xy_peers] + [sibling]
+    peers = [along_z(d) for d in range(1, NZ)] + [along_y(d) for d in range(1, NY)]
+    peers += [along_xy(1, 0), along_xy(-1, 0), sibling]
     for peer in peers:
         pl.semaphore_signal(barrier, 1, device_id=peer, device_id_type=MESH)
     pl.semaphore_wait(barrier, len(peers))
@@ -247,43 +250,45 @@
             previous = opens * NONE + (1 - opens) * (t - 1)
             products[t] = product + products[previous]
 
+    def column_sum(target, jj, owner, first, last, fresh):
+        ends = [meta_s[1, g * 8 + owner * 4 + jj] for g in range(first, last)]
+        for m in range(4):
+            rows = pl.ds(m * BS, BS)
+            total = products[ends[0], rows] if fresh else target[jj, rows]
+            for end in ends[1 if fresh else 0 :]:
+                total = total + products[end, rows]
+            target[jj, rows] = total
+
+    def fold():
+        for jj in range(4):
+            column_sum(sib_send, jj, 1 - core, 0, FOLDED, True)
+            column_sum(partial, jj, core, 0, FOLDED, True)
+
+    def sib_copy(jj):
+        return remote(SEND_SIB + jj, sib_send.at[jj], sib_recv.at[jj], sibling)
+
     left_set[64] = jnp.zeros((BS, BS), BF16)
     products[NONE] = jnp.zeros((ROWS, BS), F32)
 
     done = 0
-    opened = 0
     for item in PROGRAM:
         if item < 0:
             gather_copy(-1 - item).wait_recv()
         elif item < 200:
             gather_copy(item).start()
-            opened += 1
-            if opened == 8:
-                send_slots()
         elif item < 300:
-            if item == 201:
-                forward_slots()
             stage_source(item - 200)
         elif item == 300:
             multiply(done)
             done += STEP
         else:
-            sort_slots()
-
-    def column_sum(j):
-        total = products[meta_s[1, j]]
-        for g in range(1, NG):
-            total = total + products[meta_s[1, g * 8 + j]]
-        return total
-
-    def sib_copy(jj):
-        return remote(SEND_SIB + jj, sib_send.at[jj], sib_recv.at[jj], sibling)
-
-    for jj in range(4):
-        sib_send[jj] = column_sum((1 - core) * 4 + jj)
+            {400: sort_slots, 401: send_slots, 402: forward_slots, 500: fold}[item]()
+
+    for jj in range(4):
+        column_sum(sib_send, jj, 1 - core, FOLDED, NG, False)
         sib_copy(jj).start()
     for jj in range(4):
-        partial[jj] = column_sum(core * 4 + jj)
+        column_sum(partial, jj, core, FOLDED, NG, False)
 
     half = BS // 2
 
@@ -336,7 +341,7 @@
         return remote(SEND_SUM + n, sums_xy.at[0], sums_xy.at[slot], along_xy(dx, dy))
 
     def z_copy(n):
-        d = n + 1
+        d = (4, 3, 5, 2, 6, 1, 7)[n]
         return remote(SEND_SUM + 15 + n, sums_z.at[0], sums_z.at[(-d) % NZ], along_z(d))
 
     for n in range(15):
@@ -354,7 +359,7 @@
     for n in range(1, NZ):
         total = total + sums_z[n]
     meta_sum = sums_xy.at[1]
-    meta_sum[...] = total
+    meta_sum[...] = total / (NY * NZ * 4 * BS) + 1e-6
     last = pltpu.make_async_copy(meta_sum, sums, local_sem.at[13])
     last.start()
 
@@ -420,8 +425,7 @@
         left_blocks.reshape(64, BS, BS),
         right_blocks.reshape(ROWS, BS),
     )
-    rows = NY * NZ * 4 * BS
-    return (squares / (sums[:, None, :] / rows + 1e-6))[None]
+    return (squares / sums[:, None, :])[None]
 
 
 def solution(mesh):

time: 68.3 us -> 66 us (0.966)
  Pallas kernels: 65.5 us -> 63.5 us
    pallas_call x1, Pallas kernels: 65.5 us -> 63.5 us  [body(): pl.pallas_call(kernel, out_shape=(jax.ShapeDtypeStruct((4, BS, BS), F32),...]
where the time goes in v2:
time: 66 us; the launch traced here: 65.2 us
  Pallas kernels  63.5 us (96%)
  other arithmetic  1.68 us (3%)
    pallas_call x1, Pallas kernels, body(): pl.pallas_call(kernel, out_shape=(jax.ShapeDtypeStruct((4, BS, BS), F32),...  63.5 us
    broadcast_in_dim x1, other arithmetic, body(): return (squares / sums[:, None, :])[None]  1.68 us

profile of v2, /device:TPU:2, one launch (start us, length us, event | category | flops | bytes accessed | tf_op | source)
XLA Modules:
  0.0 65.2 jit_solution(17855115395922306623)
XLA Ops:
  0.0 63.5 %expand_and_sum.1 = (f32[4,128,128]{2,1,0:T(8,128)}, f32[4,128]{1,0:T(4,128)}) custom-call(s32[1,64]{1,0:T(1,128)} %left_slots.1, s32[1,4]{1,0:T(1,128)} %right_slots.1, s32[1,32]{1,0:T(1,128)} %out_slots.1, bf16[64,128,128]{2,1,0:T(8,128)(2,1)} %bitcast.4, bf16[512,128]{1,0:T(8,128)(2,1)} %bitcast.5), custom_call_target="tpu_custom_call" | custom-call | tf_op jit(solution)/shard_map/expand_and_sum/pallas_call | solution.py:384
  63.5 1.7 %divide_bitcast_fusion = f32[1,4,128,128]{3,2,1,0:T(8,128)} fusion(f32[4,128,128]{2,1,0:T(8,128)} %get-tuple-element.7, f32[4,128]{1,0:T(4,128)} %get-tuple-element.8), kind=kLoop, calls=%fused_computation | loop fusion | flops 65536 | bytes 526336 | tf_op jit(solution)/shard_map/broadcast_in_dim | solution.py:428

commit v3 on v2

--- a/solution.py
+++ b/solution.py
@@ -1,3 +1,5 @@
+import functools
+
 import jax
 import jax.numpy as jnp
 from jax import lax
@@ -18,21 +20,34 @@
 Z_INDEX = {0: 0, 1: 1, -1: 2, 2: 3, -2: 4, 3: 5, -3: 6, 4: 7}
 Y_INDEX = {0: 0, 1: 1, -1: 2, 2: 3}
 SOURCES = (
-    (0, 0), (0, 1), (0, 2), (1, 0), (2, 0), (0, 3), (1, 2), (2, 2), (1, 1), (2, 1), (0, 4), (0, 5),
-    (3, 1), (3, 2), (3, 0), (1, 4), (2, 4), (1, 3), (2, 3), (3, 4), (3, 3), (0, 6), (1, 5), (2, 5),
-    (1, 6), (2, 6), (0, 7), (3, 5), (3, 6), (1, 7), (2, 7), (3, 7),
+    (0, 0), (1, 0), (0, 1), (0, 2), (2, 1), (2, 0), (1, 1), (0, 4), (1, 2), (2, 2), (0, 3), (3, 0),
+    (3, 2), (3, 1), (2, 3), (1, 4), (2, 4), (1, 3), (0, 5), (0, 6), (3, 3), (3, 4), (2, 6), (2, 5),
+    (1, 6), (1, 5), (0, 7), (1, 7), (3, 6), (3, 5), (2, 7), (3, 7),
 )
 GROUPS = (4, 6, 8, 4, 4, 2, 2, 2)
-PROGRAM = (
-    6, 4, 0, 10, 401, 36, 32, 14, 200, 12, -5, -11, 11, 5, -7, 7, -1, 1, 16, 18, -33, -13, 13, 40,
-    -37, 201, 37, -15, 402, 202, -6, 33, -12, 44, -8, 8, -2, 20, 22, 2, -41, -19, -38, 203, 38, 48,
-    -17, 52, 400, -34, 15, 204, -45, 205, 206, 19, 41, 45, 17, -14, 207, -3, 3, -9, -23, 34, 23,
-    300, -16, -21, 21, 300, 208, -39, 24, 26, 209, 300, -49, 9, -53, 210, 49, -20, 211, -18, 53,
-    300, 212, 300, 213, -42, 214, 215, 42, 216, -4, -24, -22, -46, 46, 217, 39, 300, 218, -10, 28,
-    30, 300, 300, -50, 219, 50, 300, -54, 54, -35, -27, 35, 27, 220, 221, 300, -25, 25, 300, -47,
-    -43, 222, 223, 224, -31, 47, 43, 31, 225, 300, -40, -29, -51, 300, -55, 29, -28, -36, 51, 55,
-    500, 226, -26, 227, 228, 300, -48, -44, -32, 229, 300, -52, -56, 230, -30, 231, 300,
+PROGRAMS = (
+    (
+        0, 13, 8, 200, 5, 999, 16, 20, 54, 48, -14, -15, 15, -6, -7, 7, 60, 89, -50, 65, -55, -56,
+        -49, 91, -81, 999, -85, -16, -8, 70, 90, 56, 75, 50, 999, -61, -66, 66, 61, 94, -71, 200,
+        200, -23, -86, -57, -19, 200, 999, 200, -82, 71, -51, 92, -76, 97, 999, 200, 200, 76, 200,
+        200, 200, 51, 57, 999, 999, 200, 999, -29, -26, -87, 200, 200, 200, -62, 62, -67, 95, 200,
+        67, 200, 200, 200, 999, -83, -72, -35, 999, 72, -77, 77, -32, -84, 98, 999, -52, -58, 93,
+        52, 200, 200, 53, 200, 58, 200, 59, 999, 999, -63, 64, 63, -68, 96, 68, 999, 69, -73, 74,
+        -88, -78, 73, -53, 78, -59, 79, 200, 200, 200, 200, 999, 999, 99, -41, 999, 200, -89, -69,
+        -64, -38, -79, 200, 999, -47, 200, -44, 200, 200, -74, 200, 999, 999,
+    ),
+    (
+        1, 999, 14, 6, 49, 9, 17, 21, 55, -9, -1, -2, 2, -10, 10, 27, 24, 999, 200, -21, -17, 84,
+        -18, 22, 80, -11, -3, 81, 18, -22, 30, 33, -92, 3, 11, -28, -90, 200, -25, 29, 85, 25, 19,
+        26, 200, 200, 28, 999, 999, -95, 23, 999, 200, -4, 200, -34, -12, 12, 34, -31, 4, 31, -93,
+        86, 32, 200, -91, 200, -30, 39, -98, 200, 82, -20, 200, 36, 200, 35, 999, 999, 999, -24,
+        -27, 200, 200, -13, -5, 45, 200, 83, 42, -33, -96, 200, 200, 200, 200, 999, 999, 999, 999,
+        -99, -40, 40, -94, 200, 200, 41, -36, 200, 200, -37, 87, 37, 999, 38, 999, -46, -54, 47,
+        -43, 46, 43, -60, -97, 200, 200, 200, 88, 200, 44, 999, 999, 999, -75, -42, -70, -100, 200,
+        -48, -65, -39, 200, 200, -45, -80, 200, 200, 200, 999, 999, 999,
+    ),
 )
+SHARED = (401, 402, 400) + (300,) * 13 + (500,) + (300,) * 3
 STEP = 8
 NG = len(GROUPS)
 FOLDED = 5
@@ -45,7 +60,7 @@
 
 
 def gather_copies():
-    copies = []
+    plans = {}
 
     def part(kind, sign, whole):
         size, cut = (A_ROWS, A_CUT) if kind == 0 else (B_ROWS, B_CUT)
@@ -53,29 +68,60 @@
             return 0, size
         return (0, cut) if sign == 1 else (cut, size - cut)
 
+    def plan(key, kind, axis, sign, d, other, form):
+        index, count = ((Y_INDEX, NY), (Z_INDEX, NZ))[axis]
+        src = (index[-sign * (d - 1)], 1)
+        dst = (index[wrap(-sign * d, count)], 1)
+        first_axis = 0 if kind == 0 else 1
+        order = (lambda v: (v, other)) if axis == first_axis else (lambda v: (other, v))
+        plans[key] = dict(
+            kind=kind, axis=axis, sign=sign, src=order(src), dst=order(dst),
+            rows=part(kind, sign, d < count // 2), form=form,
+        )
+
     for sign in (1, -1):
         for d in range(1, 5):
-            src = ((0, 1), (Z_INDEX[-sign * (d - 1)], 1))
-            dst = ((0, 1), (Z_INDEX[wrap(-sign * d, NZ)], 1))
-            copies.append((0, 1, sign, src, dst) + part(0, sign, d < 4) + (d == 1,))
+            plan(("Az", sign, d), 0, 1, sign, d, (0, 1), "own" if d == 1 else "pass")
         for d in (1, 2):
-            src = ((0, 1), (Y_INDEX[-sign * (d - 1)], 1))
-            dst = ((0, 1), (Y_INDEX[wrap(-sign * d, NY)], 1))
-            copies.append((1, 0, sign, src, dst) + part(1, sign, d < 2) + (d == 1,))
-    for first, count in ((0, 1), (1, 2), (3, 2), (5, 2), (7, 1)):
+            plan(("By", sign, d), 1, 0, sign, d, (0, 1), "own" if d == 1 else "pass")
+    a_waves = ((0, 1), (1, 2), (3, 2), (5, 2), (7, 1))
+    b_waves = ((0, 1), (1, 2), (3, 1))
+    for w, wave in enumerate(a_waves):
         for sign in (1, -1):
             for d in (1, 2):
-                src = ((Y_INDEX[-sign * (d - 1)], 1), (first, count))
-                dst = ((Y_INDEX[wrap(-sign * d, NY)], 1), (first, count))
-                own = first == 0 and d == 1
-                copies.append((0, 0, sign, src, dst) + part(0, sign, d < 2) + (own,))
-    for first, count in ((0, 1), (1, 2), (3, 1)):
+                form = "last" if d == 2 else "pass" if w else "own"
+                plan(("Ay", w, sign, d), 0, 0, sign, d, wave, form)
+    for v, wave in enumerate(b_waves):
         for sign in (1, -1):
             for d in range(1, 5):
-                src = ((Z_INDEX[-sign * (d - 1)], 1), (first, count))
-                dst = ((Z_INDEX[wrap(-sign * d, NZ)], 1), (first, count))
-                own = first == 0 and d == 1
-                copies.append((1, 1, sign, src, dst) + part(1, sign, d < 4) + (own,))
+                form = "last" if d == 4 else "pass" if v or d > 1 else "own"
+                plan(("Bz", v, sign, d), 1, 1, sign, d, wave, form)
+    copies = []
+    for p in plans.values():
+        agent = 1 - p["kind"]
+        if p["form"] == "own":
+            copies += [dict(p, ex=c, rc=agent, lay=c) for c in (0, 1)]
+        elif p["form"] == "last":
+            copies += [dict(p, ex=agent, rc=c, lay=c) for c in (0, 1)]
+        else:
+            copies.append(dict(p, ex=agent, rc=agent, lay=2))
+
+    def push(kind, where):
+        agent = 1 - kind
+        rows = (0, A_ROWS if kind == 0 else B_ROWS)
+        copies.append(
+            dict(kind=kind, src=where, dst=where, rows=rows, form="push", ex=agent, rc=1 - agent, lay=1 - agent)
+        )
+
+    for wave in a_waves[1:]:
+        push(0, ((0, 1), wave))
+    for wave in a_waves:
+        push(0, ((1, 2), wave))
+    push(1, ((0, 1), (1, 2)))
+    push(1, ((0, 1), (3, 1)))
+    for wave in b_waves:
+        for first in (1, 3, 5):
+            push(1, ((first, 2), wave))
     return copies
 
 
@@ -97,20 +143,29 @@
 def kernel(
     left_slots, right_slots, out_slots, left, right, squares, sums,
     left_set, gather_a, gather_b, stage, products, slots_row, slots, meta, meta_s,
-    left_s, right_s, out_s, sib_send, sib_recv, partial, half_recv, full_recv,
+    left_s, right_s, out_s, sib_send, sib_recv, partial, half_send, near_send, full_send,
+    half_recv, near_recv, full_recv,
     sums_xy, sums_z, squared, send_sem, recv_sem, local_sem,
 ):
     y, z, layer = lax.axis_index("row"), lax.axis_index("col"), lax.axis_index("layer")
-    x, core = layer // 2, lax.rem(layer, 2)
+    x, core = layer >> 1, layer & 1
+
+    ys = [y] + [(y + d) & (NY - 1) for d in range(1, NY)]
+    zs = [z] + [(z + d) & (NZ - 1) for d in range(1, NZ)]
+    xs = [x] + [(x + d) & (NX - 1) for d in range(1, NX)]
+    layers = [layer] + [xs[d] * 2 + core for d in range(1, NX)]
 
     def along_y(d):
-        return (lax.rem(y + (d % NY), NY), z, layer)
+        return (ys[d % NY], z, layer)
 
     def along_z(d):
-        return (y, lax.rem(z + (d % NZ), NZ), layer)
+        return (y, zs[d % NZ], layer)
 
     def along_xy(dx, dy):
-        return (lax.rem(y + dy % NY, NY), z, lax.rem(x + dx % NX, NX) * 2 + core)
+        return (ys[dy % NY], z, layers[dx % NX])
+
+    def at_core(device, c):
+        return (device[0], device[1], x * 2 + c)
 
     sibling = (y, z, x * 2 + (1 - core))
     xy_peers = [(dx, dy) for dx in range(NX) for dy in range(NY) if dx or dy]
@@ -131,6 +186,7 @@
     barrier = pltpu.get_barrier_semaphore()
     peers = [along_z(d) for d in range(1, NZ)] + [along_y(d) for d in range(1, NY)]
     peers += [along_xy(1, 0), along_xy(-1, 0), sibling]
+    peers += [at_core(p, 1 - core) for p in (along_z(1), along_z(-1), along_y(1), along_y(-1))]
     for peer in peers:
         pl.semaphore_signal(barrier, 1, device_id=peer, device_id_type=MESH)
     pl.semaphore_wait(barrier, len(peers))
@@ -142,17 +198,25 @@
         )
 
     def gather_copy(n):
-        kind, axis, sign, src, dst, row, rows, own = COPIES[n]
-        buffer = gather_a if kind == 0 else gather_b
+        copy = COPIES[n]
+        buffer = (gather_a, gather_b)[copy["kind"]]
+        row, rows = copy["rows"]
 
         def place(where):
-            (p, _), (q, qn) = where
-            if qn == 1:
-                return buffer.at[p, q, pl.ds(row, rows)]
-            return buffer.at[p, pl.ds(q, qn), pl.ds(row, rows)]
-
-        source = right.at[pl.ds((0 if kind == 0 else A_ROWS) + row, rows)] if own else place(src)
-        return remote(n, source, place(dst), along_z(sign) if axis else along_y(sign))
+            index = [first if count == 1 else pl.ds(first, count) for first, count in where]
+            lay = pl.ds(0, 2) if copy["lay"] == 2 else copy["lay"]
+            return buffer.at[index[0], index[1], lay, pl.ds(row, rows)]
+
+        if copy["form"] == "push":
+            device = sibling
+        else:
+            along = along_z if copy["axis"] else along_y
+            device = at_core(along(copy["sign"]), copy["rc"])
+        if copy["form"] == "own":
+            source = right.at[pl.ds((0 if copy["kind"] == 0 else A_ROWS) + row, rows)]
+        else:
+            source = place(copy["src"])
+        return remote(n, source, place(copy["dst"]), device)
 
     def small_copy(n):
         if n < 7:
@@ -222,17 +286,17 @@
         for copy in local[2:]:
             copy.wait()
 
-    def stage_source(p):
+    def stage_source(p, c):
         if p == 0:
             return
         yi, zi = SOURCES[p]
         a_tail = A_ROWS - 2 * BS
         b_head = BS - a_tail
-        stage[4 * p] = gather_a[yi, zi, pl.ds(0, BS)]
-        stage[4 * p + 1] = gather_a[yi, zi, pl.ds(BS, BS)]
-        stage[4 * p + 2, pl.ds(0, a_tail)] = gather_a[yi, zi, pl.ds(2 * BS, a_tail)]
-        stage[4 * p + 2, pl.ds(a_tail, b_head)] = gather_b[zi, yi, pl.ds(0, b_head)]
-        stage[4 * p + 3] = gather_b[zi, yi, pl.ds(b_head, BS)]
+        stage[4 * p] = gather_a[yi, zi, c, pl.ds(0, BS)]
+        stage[4 * p + 1] = gather_a[yi, zi, c, pl.ds(BS, BS)]
+        stage[4 * p + 2, pl.ds(0, a_tail)] = gather_a[yi, zi, c, pl.ds(2 * BS, a_tail)]
+        stage[4 * p + 2, pl.ds(a_tail, b_head)] = gather_b[zi, yi, c, pl.ds(0, b_head)]
+        stage[4 * p + 3] = gather_b[zi, yi, c, pl.ds(b_head, BS)]
 
     def multiply(start):
         for t in range(start, start + STEP):
@@ -241,7 +305,7 @@
             k, j = slot >> 3, slot & 7
             chosen = []
             for m in range(4):
-                r = out_s[0, lax.rem(x + m, NX) * 8 + j] >> 3
+                r = out_s[0, xs[m] * 8 + j] >> 3
                 at = r * 32 + k
                 chosen.append(left_set[meta_s[2 + (at >> 7), at & 127]])
             product = jnp.dot(
@@ -270,19 +334,40 @@
     left_set[64] = jnp.zeros((BS, BS), BF16)
     products[NONE] = jnp.zeros((ROWS, BS), F32)
 
+    def run(items, staged, c):
+        for item in items:
+            if item == 200:
+                stage_source(staged, c)
+                staged += 1
+            elif item < 0:
+                gather_copy(-1 - item).wait_recv()
+            else:
+                gather_copy(item).start()
+
+    def sections(c):
+        found, items, staged = [], [], 0
+        for item in PROGRAMS[c] + (999,):
+            if item == 999:
+                found.append((items, staged))
+                staged += items.count(200)
+                items = []
+            else:
+                items.append(item)
+        return found
+
     done = 0
-    for item in PROGRAM:
-        if item < 0:
-            gather_copy(-1 - item).wait_recv()
-        elif item < 200:
-            gather_copy(item).start()
-        elif item < 300:
-            stage_source(item - 200)
-        elif item == 300:
+    for n, (first, second) in enumerate(zip(sections(0), sections(1))):
+        if first[0]:
+            pl.when(core == 0)(functools.partial(run, *first, 0))
+        if second[0]:
+            pl.when(core == 1)(functools.partial(run, *second, 1))
+        if n == len(SHARED):
+            break
+        if SHARED[n] == 300:
             multiply(done)
             done += STEP
         else:
-            {400: sort_slots, 401: send_slots, 402: forward_slots, 500: fold}[item]()
+            {400: sort_slots, 401: send_slots, 402: forward_slots, 500: fold}[SHARED[n]]()
 
     for jj in range(4):
         column_sum(sib_send, jj, 1 - core, FOLDED, NG, False)
@@ -292,43 +377,68 @@
 
     half = BS // 2
 
+    def exponent(value):
+        largest = jnp.max(jnp.abs(value), axis=0, keepdims=True)
+        return jnp.ceil(jnp.log2(jnp.maximum(largest, 1e-30)))
+
+    def encode(value, power):
+        scaled = jnp.round(value * jnp.exp2(15.0 - power))
+        return jnp.clip(scaled, -32767.0, 32767.0).astype(I32).astype(jnp.int16)
+
+    def decode(code, power):
+        return code.astype(I32).astype(F32) * jnp.exp2(power - 15.0)
+
+    def powers(first, second):
+        rows = [jnp.broadcast_to(p.astype(I32), (8, BS)) for p in (first, second)]
+        return jnp.concatenate(rows, axis=0).astype(jnp.int16)
+
+    def read_powers(ref, side, jj):
+        rows = ref[side, jj, pl.ds(half, 16)].astype(I32).astype(F32)
+        return rows[0:1], rows[8:9]
+
     def x_copy(jj, what):
-        number = SEND_X + jj * 6 + what
-        forth = what % 2 == 0
-        side = 0 if forth else 1
-        device = along_xy(1, 0) if forth else along_xy(-1, 0)
-        if what < 2:
-            src = partial.at[jj, pl.ds(2 * BS + side * half, half)]
-            dst = half_recv.at[side, jj]
-        else:
-            base = BS if forth else 3 * BS
-            row = (half if forth else 0) if what < 4 else (0 if forth else half)
-            src = partial.at[jj, pl.ds(base + row, half)]
-            dst = full_recv.at[side, jj, pl.ds(row, half)]
-        return remote(number, src, dst, device)
+        side, stage_of = what % 2, what // 2
+        src = (half_send, near_send, full_send)[stage_of].at[side, jj]
+        dst = (half_recv, near_recv, full_recv)[stage_of].at[side, jj]
+        device = along_xy(1, 0) if side == 0 else along_xy(-1, 0)
+        return remote(SEND_X + jj * 6 + what, src, dst, device)
 
     for jj in range(4):
         sib_copy(jj).wait_recv()
         partial[jj] = partial[jj] + sib_recv[jj]
-        x_copy(jj, 0).start()
-        x_copy(jj, 1).start()
+        for side in range(2):
+            far = partial[jj, pl.ds(2 * BS + side * half, half)]
+            near = partial[jj, pl.ds((BS + half) if side == 0 else 3 * BS, half)]
+            far_power, near_power = exponent(far), exponent(near)
+            half_send[side, jj, pl.ds(0, half)] = encode(far, far_power)
+            half_send[side, jj, pl.ds(half, 16)] = powers(far_power, near_power)
+            x_copy(jj, side).start()
+            near_send[side, jj] = encode(near, near_power)
     for jj in range(4):
         x_copy(jj, 2).start()
         x_copy(jj, 3).start()
     for jj in range(4):
-        x_copy(jj, 0).wait_recv()
-        partial[jj, pl.ds(BS, half)] = partial[jj, pl.ds(BS, half)] + half_recv[0, jj]
-        x_copy(jj, 4).start()
-        x_copy(jj, 1).wait_recv()
-        partial[jj, pl.ds(3 * BS + half, half)] = (
-            partial[jj, pl.ds(3 * BS + half, half)] + half_recv[1, jj]
-        )
-        x_copy(jj, 5).start()
+        for side in range(2):
+            x_copy(jj, side).wait_recv()
+            power, _ = read_powers(half_recv, side, jj)
+            own = partial[jj, pl.ds(BS if side == 0 else 3 * BS + half, half)]
+            value = own + decode(half_recv[side, jj, pl.ds(0, half)], power)
+            power = exponent(value)
+            full_send[side, jj, pl.ds(0, half)] = encode(value, power)
+            full_send[side, jj, pl.ds(half, 16)] = powers(power, power)
+            x_copy(jj, 4 + side).start()
     stores = []
     for jj in range(4):
         for what in (2, 3, 4, 5):
             x_copy(jj, what).wait_recv()
-        total = partial[jj, pl.ds(0, BS)] + full_recv[0, jj] + full_recv[1, jj]
+        total = []
+        for part in range(2):
+            value = partial[jj, pl.ds(part * half, half)]
+            _, power = read_powers(half_recv, 1 - part, jj)
+            value = value + decode(near_recv[1 - part, jj], power)
+            power, _ = read_powers(full_recv, part, jj)
+            total.append(value + decode(full_recv[part, jj, pl.ds(0, half)], power))
+        total = jnp.concatenate(total, axis=0)
         square = total * total
         squared[jj] = square
         stores.append(pltpu.make_async_copy(squared.at[jj], squares.at[jj], local_sem.at[9 + jj]))
@@ -363,8 +473,13 @@
     last = pltpu.make_async_copy(meta_sum, sums, local_sem.at[13])
     last.start()
 
-    for n in range(len(COPIES)):
-        gather_copy(n).wait_send()
+    def finish(c):
+        for n, copy in enumerate(COPIES):
+            if copy["ex"] == c:
+                gather_copy(n).wait_send()
+
+    pl.when(core == 0)(functools.partial(finish, 0))
+    pl.when(core == 1)(functools.partial(finish, 1))
     for n in range(N_SMALL):
         small_copy(n).wait_send()
     for jj in range(4):
@@ -391,8 +506,8 @@
         out_specs=(any_spec, any_spec),
         scratch_shapes=[
             pltpu.VMEM((65, BS, BS), BF16),
-            pltpu.VMEM((NY, NZ, A_ROWS, BS), BF16),
-            pltpu.VMEM((NZ, NY, B_ROWS, BS), BF16),
+            pltpu.VMEM((NY, NZ, 2, A_ROWS, BS), BF16),
+            pltpu.VMEM((NZ, NY, 2, B_ROWS, BS), BF16),
             pltpu.VMEM((32 * 4, BS, BS), BF16),
             pltpu.VMEM((NONE + 1, ROWS, BS), F32),
             pltpu.VMEM((1, BS), I32),
@@ -405,8 +520,12 @@
             pltpu.VMEM((4, ROWS, BS), F32),
             pltpu.VMEM((4, ROWS, BS), F32),
             pltpu.VMEM((4, ROWS, BS), F32),
-            pltpu.VMEM((2, 4, BS // 2, BS), F32),
-            pltpu.VMEM((2, 4, BS, BS), F32),
+            pltpu.VMEM((2, 4, BS // 2 + 16, BS), jnp.int16),
+            pltpu.VMEM((2, 4, BS // 2, BS), jnp.int16),
+            pltpu.VMEM((2, 4, BS // 2 + 16, BS), jnp.int16),
+            pltpu.VMEM((2, 4, BS // 2 + 16, BS), jnp.int16),
+            pltpu.VMEM((2, 4, BS // 2, BS), jnp.int16),
+            pltpu.VMEM((2, 4, BS // 2 + 16, BS), jnp.int16),
             pltpu.VMEM((16, 4, BS), F32),
             pltpu.VMEM((NZ, 4, BS), F32),
             pltpu.VMEM((4, BS, BS), F32),

time: 66 us -> 62.5 us (0.947); the launches traced: 65.2 us -> 62.4 us
  Pallas kernels: 63.5 us -> 60.7 us
    pallas_call x1, Pallas kernels: 63.5 us -> 60.7 us  [body(): pl.pallas_call(kernel, out_shape=(jax.ShapeDtypeStruct((4, BS, BS), F32),...]
where the time goes in v3:
time: 62.5 us; the launch traced here: 62.4 us
  Pallas kernels  60.7 us (97%)
  other arithmetic  1.68 us (3%)
    pallas_call x1, Pallas kernels, body(): pl.pallas_call(kernel, out_shape=(jax.ShapeDtypeStruct((4, BS, BS), F32),...  60.7 us
    broadcast_in_dim x1, other arithmetic, body(): return (squares / sums[:, None, :])[None]  1.68 us

profile of v3, /device:TPU:2, one launch (start us, length us, event | category | flops | bytes accessed | tf_op | source)
XLA Modules:
  0.0 62.4 jit_solution(2830162560598841640)
XLA Ops:
  0.0 60.7 %expand_and_sum.1 = (f32[4,128,128]{2,1,0:T(8,128)}, f32[4,128]{1,0:T(4,128)}) custom-call(s32[1,64]{1,0:T(1,128)} %left_slots.1, s32[1,4]{1,0:T(1,128)} %right_slots.1, s32[1,32]{1,0:T(1,128)} %out_slots.1, bf16[64,128,128]{2,1,0:T(8,128)(2,1)} %bitcast.4, bf16[512,128]{1,0:T(8,128)(2,1)} %bitcast.5), custom_call_target="tpu_custom_call" | custom-call | tf_op jit(solution)/shard_map/expand_and_sum/pallas_call | solution.py:499
  60.8 1.7 %divide_bitcast_fusion = f32[1,4,128,128]{3,2,1,0:T(8,128)} fusion(f32[4,128,128]{2,1,0:T(8,128)} %get-tuple-element.7, f32[4,128]{1,0:T(4,128)} %get-tuple-element.8), kind=kLoop, calls=%fused_computation | loop fusion | flops 65536 | bytes 526336 | tf_op jit(solution)/shard_map/broadcast_in_dim | solution.py:547

commit v4 on v3

--- a/solution.py
+++ b/solution.py
@@ -128,7 +128,7 @@
 COPIES = gather_copies()
 N_SMALL = 7 + 3
 N_X = 4 * 6
-N_SUM = 15 + 7
+N_SUM = 2
 SEND_SMALL = len(COPIES)
 SEND_SIB = SEND_SMALL + N_SMALL
 SEND_X = SEND_SIB + 4
@@ -142,13 +142,14 @@
 
 def kernel(
     left_slots, right_slots, out_slots, left, right, squares, sums,
-    left_set, gather_a, gather_b, stage, products, slots_row, slots, meta, meta_s,
+    left_set, gather_a, gather_b, stage, products_0, products_1, products_2, products_3, slots_row, slots, meta, meta_s,
     left_s, right_s, out_s, sib_send, sib_recv, partial, half_send, near_send, full_send,
     half_recv, near_recv, full_recv,
-    sums_xy, sums_z, squared, send_sem, recv_sem, local_sem,
+    sums_xy, sums_z, scale, squared, send_sem, recv_sem, local_sem,
 ):
     y, z, layer = lax.axis_index("row"), lax.axis_index("col"), lax.axis_index("layer")
     x, core = layer >> 1, layer & 1
+    products = (products_0, products_1, products_2, products_3)
 
     ys = [y] + [(y + d) & (NY - 1) for d in range(1, NY)]
     zs = [z] + [(z + d) & (NZ - 1) for d in range(1, NZ)]
@@ -312,15 +313,17 @@
                 jnp.concatenate(chosen, axis=0), stage[block], preferred_element_type=F32
             )
             previous = opens * NONE + (1 - opens) * (t - 1)
-            products[t] = product + products[previous]
+            for m in range(4):
+                rows = product[m * BS : (m + 1) * BS]
+                products[m][t] = rows + products[m][previous]
 
     def column_sum(target, jj, owner, first, last, fresh):
         ends = [meta_s[1, g * 8 + owner * 4 + jj] for g in range(first, last)]
         for m in range(4):
             rows = pl.ds(m * BS, BS)
-            total = products[ends[0], rows] if fresh else target[jj, rows]
+            total = products[m][ends[0]] if fresh else target[jj, rows]
             for end in ends[1 if fresh else 0 :]:
-                total = total + products[end, rows]
+                total = total + products[m][end]
             target[jj, rows] = total
 
     def fold():
@@ -332,7 +335,8 @@
         return remote(SEND_SIB + jj, sib_send.at[jj], sib_recv.at[jj], sibling)
 
     left_set[64] = jnp.zeros((BS, BS), BF16)
-    products[NONE] = jnp.zeros((ROWS, BS), F32)
+    for m in range(4):
+        products[m][NONE] = jnp.zeros((BS, BS), F32)
 
     def run(items, staged, c):
         for item in items:
@@ -396,6 +400,15 @@
         rows = ref[side, jj, pl.ds(half, 16)].astype(I32).astype(F32)
         return rows[0:1], rows[8:9]
 
+    def drain(c, first, last):
+        sent = [n for n, copy in enumerate(COPIES) if copy["ex"] == c]
+        for n in sent[first:last]:
+            gather_copy(n).wait_send()
+
+    def drain_gather(first, last):
+        pl.when(core == 0)(functools.partial(drain, 0, first, last))
+        pl.when(core == 1)(functools.partial(drain, 1, first, last))
+
     def x_copy(jj, what):
         side, stage_of = what % 2, what // 2
         src = (half_send, near_send, full_send)[stage_of].at[side, jj]
@@ -403,6 +416,7 @@
         device = along_xy(1, 0) if side == 0 else along_xy(-1, 0)
         return remote(SEND_X + jj * 6 + what, src, dst, device)
 
+    drain_gather(0, 16)
     for jj in range(4):
         sib_copy(jj).wait_recv()
         partial[jj] = partial[jj] + sib_recv[jj]
@@ -417,6 +431,7 @@
     for jj in range(4):
         x_copy(jj, 2).start()
         x_copy(jj, 3).start()
+    drain_gather(16, len(COPIES))
     for jj in range(4):
         for side in range(2):
             x_copy(jj, side).wait_recv()
@@ -427,6 +442,12 @@
             full_send[side, jj, pl.ds(0, half)] = encode(value, power)
             full_send[side, jj, pl.ds(half, 16)] = powers(power, power)
             x_copy(jj, 4 + side).start()
+    for n in range(N_SMALL):
+        small_copy(n).wait_send()
+    for jj in range(4):
+        sib_copy(jj).wait_send()
+        for what in range(4):
+            x_copy(jj, what).wait_send()
     stores = []
     for jj in range(4):
         for what in (2, 3, 4, 5):
@@ -448,49 +469,37 @@
     def xy_copy(n):
         dx, dy = xy_peers[n]
         slot = ((-dx) % NX) * NY + (-dy) % NY
-        return remote(SEND_SUM + n, sums_xy.at[0], sums_xy.at[slot], along_xy(dx, dy))
+        return remote(SEND_SUM, sums_xy.at[0], sums_xy.at[slot], along_xy(dx, dy))
 
     def z_copy(n):
         d = (4, 3, 5, 2, 6, 1, 7)[n]
-        return remote(SEND_SUM + 15 + n, sums_z.at[0], sums_z.at[(-d) % NZ], along_z(d))
-
+        return remote(SEND_SUM + 1, sums_z.at[0], sums_z.at[(-d) % NZ], along_z(d))
+
+    xy_all = sums_xy.at[pl.ds(1, 15)]
+    z_all = sums_z.at[pl.ds(1, 7)]
+    xy_round = remote(SEND_SUM, xy_all, xy_all, along_xy(1, 0))
+    z_round = remote(SEND_SUM + 1, z_all, z_all, along_z(1))
     for n in range(15):
         xy_copy(n).start()
     total = sums_xy[0]
-    for n in range(15):
-        xy_copy(n).wait_recv()
+    for jj in range(4):
+        x_copy(jj, 4).wait_send()
+        x_copy(jj, 5).wait_send()
+        stores[jj].wait()
+    xy_round.wait_recv()
     for n in range(1, 16):
         total = total + sums_xy[n]
     sums_z[0] = total
     for n in range(7):
         z_copy(n).start()
-    for n in range(7):
-        z_copy(n).wait_recv()
+    xy_round.wait_send()
+    z_round.wait_recv()
     for n in range(1, NZ):
         total = total + sums_z[n]
-    meta_sum = sums_xy.at[1]
-    meta_sum[...] = total / (NY * NZ * 4 * BS) + 1e-6
-    last = pltpu.make_async_copy(meta_sum, sums, local_sem.at[13])
+    scale[...] = total / (NY * NZ * 4 * BS) + 1e-6
+    last = pltpu.make_async_copy(scale, sums, local_sem.at[13])
     last.start()
-
-    def finish(c):
-        for n, copy in enumerate(COPIES):
-            if copy["ex"] == c:
-                gather_copy(n).wait_send()
-
-    pl.when(core == 0)(functools.partial(finish, 0))
-    pl.when(core == 1)(functools.partial(finish, 1))
-    for n in range(N_SMALL):
-        small_copy(n).wait_send()
-    for jj in range(4):
-        sib_copy(jj).wait_send()
-        for what in range(6):
-            x_copy(jj, what).wait_send()
-        stores[jj].wait()
-    for n in range(15):
-        xy_copy(n).wait_send()
-    for n in range(7):
-        z_copy(n).wait_send()
+    z_round.wait_send()
     last.wait()
 
 
@@ -509,7 +518,10 @@
             pltpu.VMEM((NY, NZ, 2, A_ROWS, BS), BF16),
             pltpu.VMEM((NZ, NY, 2, B_ROWS, BS), BF16),
             pltpu.VMEM((32 * 4, BS, BS), BF16),
-            pltpu.VMEM((NONE + 1, ROWS, BS), F32),
+            pltpu.VMEM((NONE + 1, BS, BS), F32),
+            pltpu.VMEM((NONE + 1, BS, BS), F32),
+            pltpu.VMEM((NONE + 1, BS, BS), F32),
+            pltpu.VMEM((NONE + 1, BS, BS), F32),
             pltpu.VMEM((1, BS), I32),
             pltpu.VMEM((NY, NZ, 1, BS), I32),
             pltpu.VMEM((8, BS), I32),
@@ -528,6 +540,7 @@
             pltpu.VMEM((2, 4, BS // 2 + 16, BS), jnp.int16),
             pltpu.VMEM((16, 4, BS), F32),
             pltpu.VMEM((NZ, 4, BS), F32),
+            pltpu.VMEM((4, BS), F32),
             pltpu.VMEM((4, BS, BS), F32),
             pltpu.SemaphoreType.DMA((N_SEM,)),
             pltpu.SemaphoreType.DMA((N_SEM,)),

time: 62.5 us -> 61.5 us (0.984)
  Pallas kernels: 60.7 us -> 59.8 us
    pallas_call x1, Pallas kernels: 60.7 us -> 59.8 us  [body(): pl.pallas_call(kernel, out_shape=(jax.ShapeDtypeStruct((4, BS, BS), F32),...]
where the time goes in v4:
time: 61.5 us
  Pallas kernels  59.8 us (97%)
  other arithmetic  1.68 us (3%)
    pallas_call x1, Pallas kernels, body(): pl.pallas_call(kernel, out_shape=(jax.ShapeDtypeStruct((4, BS, BS), F32),...  59.8 us
    broadcast_in_dim x1, other arithmetic, body(): return (squares / sums[:, None, :])[None]  1.68 us

profile of v4, /device:TPU:2, one launch (start us, length us, event | category | flops | bytes accessed | tf_op | source)
XLA Modules:
  0.0 61.5 jit_solution(13946238335195039979)
XLA Ops:
  0.0 59.8 %expand_and_sum.1 = (f32[4,128,128]{2,1,0:T(8,128)}, f32[4,128]{1,0:T(4,128)}) custom-call(s32[1,64]{1,0:T(1,128)} %left_slots.1, s32[1,4]{1,0:T(1,128)} %right_slots.1, s32[1,32]{1,0:T(1,128)} %out_slots.1, bf16[64,128,128]{2,1,0:T(8,128)(2,1)} %bitcast.4, bf16[512,128]{1,0:T(8,128)(2,1)} %bitcast.5), custom_call_target="tpu_custom_call" | custom-call | tf_op jit(solution)/shard_map/expand_and_sum/pallas_call | solution.py:508
  59.8 1.7 %divide_bitcast_fusion = f32[1,4,128,128]{3,2,1,0:T(8,128)} fusion(f32[4,128,128]{2,1,0:T(8,128)} %get-tuple-element.7, f32[4,128]{1,0:T(4,128)} %get-tuple-element.8), kind=kLoop, calls=%fused_computation | loop fusion | flops 65536 | bytes 526336 | tf_op jit(solution)/shard_map/broadcast_in_dim | solution.py:560

commit v5 on v4

--- a/solution.py
+++ b/solution.py
@@ -20,31 +20,31 @@
 Z_INDEX = {0: 0, 1: 1, -1: 2, 2: 3, -2: 4, 3: 5, -3: 6, 4: 7}
 Y_INDEX = {0: 0, 1: 1, -1: 2, 2: 3}
 SOURCES = (
-    (0, 0), (1, 0), (0, 1), (0, 2), (2, 1), (2, 0), (1, 1), (0, 4), (1, 2), (2, 2), (0, 3), (3, 0),
-    (3, 2), (3, 1), (2, 3), (1, 4), (2, 4), (1, 3), (0, 5), (0, 6), (3, 3), (3, 4), (2, 6), (2, 5),
-    (1, 6), (1, 5), (0, 7), (1, 7), (3, 6), (3, 5), (2, 7), (3, 7),
+    (0, 0), (1, 2), (2, 2), (2, 1), (1, 0), (0, 1), (2, 0), (0, 2), (0, 3), (0, 4), (1, 1), (3, 1),
+    (3, 0), (1, 3), (2, 4), (3, 2), (1, 4), (2, 3), (0, 6), (0, 5), (3, 3), (3, 4), (2, 5), (2, 6),
+    (1, 6), (1, 5), (0, 7), (3, 6), (3, 5), (2, 7), (1, 7), (3, 7),
 )
 GROUPS = (4, 6, 8, 4, 4, 2, 2, 2)
 PROGRAMS = (
     (
-        0, 13, 8, 200, 5, 999, 16, 20, 54, 48, -14, -15, 15, -6, -7, 7, 60, 89, -50, 65, -55, -56,
-        -49, 91, -81, 999, -85, -16, -8, 70, 90, 56, 75, 50, 999, -61, -66, 66, 61, 94, -71, 200,
-        200, -23, -86, -57, -19, 200, 999, 200, -82, 71, -51, 92, -76, 97, 999, 200, 200, 76, 200,
-        200, 200, 51, 57, 999, 999, 200, 999, -29, -26, -87, 200, 200, 200, -62, 62, -67, 95, 200,
-        67, 200, 200, 200, 999, -83, -72, -35, 999, 72, -77, 77, -32, -84, 98, 999, -52, -58, 93,
-        52, 200, 200, 53, 200, 58, 200, 59, 999, 999, -63, 64, 63, -68, 96, 68, 999, 69, -73, 74,
-        -88, -78, 73, -53, 78, -59, 79, 200, 200, 200, 200, 999, 999, 99, -41, 999, 200, -89, -69,
-        -64, -38, -79, 200, 999, -47, 200, -44, 200, 200, -74, 200, 999, 999,
+        8, 5, 0, 13, 54, 999, 48, 16, 20, -6, -7, 7, -14, -15, 15, 65, 999, 89, 60, -56, -8, -50,
+        91, -55, -49, -16, 50, 56, 70, 75, -81, -66, -61, 61, 94, 200, 66, -23, -82, -85, 90, -51,
+        -19, -57, 999, -86, 51, 200, 200, 200, 57, -76, -71, 97, 92, 200, 76, 200, 200, 200, 999,
+        71, 200, 999, 200, 200, -87, 999, -29, 999, -26, -67, 67, 200, 200, -62, 62, 95, 200, 999,
+        -83, -58, 200, 200, -52, 93, 200, 200, 200, 999, -32, -77, 77, 59, -72, 72, -35, 58, 98,
+        200, 200, 53, 52, 200, 999, 999, -84, 999, 999, -68, 68, 69, -63, 96, 64, 63, -88, 999, -78,
+        79, 200, 200, 78, 200, 200, -73, 73, 99, 74, -53, 999, 999, -41, -59, -89, 999, -69, -38,
+        200, 200, 999, -44, -64, 200, 200, 200, -47, -74, -79, 999, 200, 999,
     ),
     (
-        1, 999, 14, 6, 49, 9, 17, 21, 55, -9, -1, -2, 2, -10, 10, 27, 24, 999, 200, -21, -17, 84,
-        -18, 22, 80, -11, -3, 81, 18, -22, 30, 33, -92, 3, 11, -28, -90, 200, -25, 29, 85, 25, 19,
-        26, 200, 200, 28, 999, 999, -95, 23, 999, 200, -4, 200, -34, -12, 12, 34, -31, 4, 31, -93,
-        86, 32, 200, -91, 200, -30, 39, -98, 200, 82, -20, 200, 36, 200, 35, 999, 999, 999, -24,
-        -27, 200, 200, -13, -5, 45, 200, 83, 42, -33, -96, 200, 200, 200, 200, 999, 999, 999, 999,
-        -99, -40, 40, -94, 200, 200, 41, -36, 200, 200, -37, 87, 37, 999, 38, 999, -46, -54, 47,
-        -43, 46, 43, -60, -97, 200, 200, 200, 88, 200, 44, 999, 999, 999, -75, -42, -70, -100, 200,
-        -48, -65, -39, 200, 200, -45, -80, 200, 200, 200, 999, 999, 999,
+        9, 999, 6, 1, 14, 200, 49, 55, 17, 21, -9, -10, 10, -1, -2, 2, 24, 27, -17, 80, -22, -21,
+        84, 999, -11, 18, -18, -3, 30, 22, 3, 33, 11, -25, 81, 23, -28, 28, 19, 26, 85, -95, 29,
+        200, 25, -92, 999, -12, -31, 200, -4, 31, -34, 34, 86, 36, 12, 200, -90, 39, 82, 999, -98,
+        200, 200, 35, 32, 4, -93, 200, 200, 999, -27, -30, -24, 200, -91, 200, 999, 200, 999, -20,
+        200, 200, 999, -96, 200, 200, 200, 200, 200, 999, -5, -13, 42, 45, 83, -94, 999, 999, 200,
+        -37, -40, 40, 87, 999, 41, -33, -36, 38, -99, 200, 37, 200, 200, 999, 999, -60, -54, -43,
+        43, 44, -46, 47, 46, -97, 88, 200, 200, 200, 200, 999, 999, 999, -39, -100, 200, -42, 200,
+        999, -48, -45, -65, 200, -70, -75, -80, 200, 200, 999, 200, 999,
     ),
 )
 SHARED = (401, 402, 400) + (300,) * 13 + (500,) + (300,) * 3
@@ -172,6 +172,12 @@
     xy_peers = [(dx, dy) for dx in range(NX) for dy in range(NY) if dx or dy]
     xy_peers.sort(key=lambda p: -min(p[0], NX - p[0]) - min(p[1], NY - p[1]))
 
+    barrier = pltpu.get_barrier_semaphore()
+    peers = [along_z(d) for d in (4, 3, 5, 2, 6, 1, 7)] + [along_y(d) for d in (2, 1, 3)]
+    peers += [along_xy(1, 0), along_xy(-1, 0), sibling]
+    peers += [at_core(p, 1 - core) for p in (along_z(1), along_z(-1), along_y(1), along_y(-1))]
+    for peer in peers:
+        pl.semaphore_signal(barrier, 1, device_id=peer, device_id_type=MESH)
     local = [
         pltpu.make_async_copy(right_slots, right_s, local_sem.at[0]),
         pltpu.make_async_copy(left_slots, left_s, local_sem.at[1]),
@@ -183,13 +189,9 @@
     ]
     for copy in local:
         copy.start()
-
-    barrier = pltpu.get_barrier_semaphore()
-    peers = [along_z(d) for d in range(1, NZ)] + [along_y(d) for d in range(1, NY)]
-    peers += [along_xy(1, 0), along_xy(-1, 0), sibling]
-    peers += [at_core(p, 1 - core) for p in (along_z(1), along_z(-1), along_y(1), along_y(-1))]
-    for peer in peers:
-        pl.semaphore_signal(barrier, 1, device_id=peer, device_id_type=MESH)
+    left_set[64] = jnp.zeros((BS, BS), BF16)
+    for m in range(4):
+        products[m][NONE] = jnp.zeros((BS, BS), F32)
     pl.semaphore_wait(barrier, len(peers))
 
     def remote(number, src, dst, device):
@@ -334,9 +336,6 @@
     def sib_copy(jj):
         return remote(SEND_SIB + jj, sib_send.at[jj], sib_recv.at[jj], sibling)
 
-    left_set[64] = jnp.zeros((BS, BS), BF16)
-    for m in range(4):
-        products[m][NONE] = jnp.zeros((BS, BS), F32)
 
     def run(items, staged, c):
         for item in items:
@@ -417,6 +416,7 @@
         return remote(SEND_X + jj * 6 + what, src, dst, device)
 
     drain_gather(0, 16)
+    near_powers = []
     for jj in range(4):
         sib_copy(jj).wait_recv()
         partial[jj] = partial[jj] + sib_recv[jj]
@@ -427,10 +427,12 @@
             half_send[side, jj, pl.ds(0, half)] = encode(far, far_power)
             half_send[side, jj, pl.ds(half, 16)] = powers(far_power, near_power)
             x_copy(jj, side).start()
-            near_send[side, jj] = encode(near, near_power)
-    for jj in range(4):
-        x_copy(jj, 2).start()
-        x_copy(jj, 3).start()
+            near_powers.append(near_power)
+    for jj in range(4):
+        for side in range(2):
+            near = partial[jj, pl.ds((BS + half) if side == 0 else 3 * BS, half)]
+            near_send[side, jj] = encode(near, near_powers[2 * jj + side])
+            x_copy(jj, 2 + side).start()
     drain_gather(16, len(COPIES))
     for jj in range(4):
         for side in range(2):

time: 61.5 us -> 61.2 us (level)
  no operation moved by 1% of the time
where the time goes in v5:
time: 61.2 us; the launch traced here: 61.1 us
  Pallas kernels  59.4 us (97%)
  other arithmetic  1.68 us (3%)
    pallas_call x1, Pallas kernels, body(): pl.pallas_call(kernel, out_shape=(jax.ShapeDtypeStruct((4, BS, BS), F32),...  59.4 us
    broadcast_in_dim x1, other arithmetic, body(): return (squares / sums[:, None, :])[None]  1.68 us

profile of v5, /device:TPU:2, one launch (start us, length us, event | category | flops | bytes accessed | tf_op | source)
XLA Modules:
  0.0 61.1 jit_solution(6889245683676933268)
XLA Ops:
  0.0 59.4 %expand_and_sum.1 = (f32[4,128,128]{2,1,0:T(8,128)}, f32[4,128]{1,0:T(4,128)}) custom-call(s32[1,64]{1,0:T(1,128)} %left_slots.1, s32[1,4]{1,0:T(1,128)} %right_slots.1, s32[1,32]{1,0:T(1,128)} %out_slots.1, bf16[64,128,128]{2,1,0:T(8,128)(2,1)} %bitcast.4, bf16[512,128]{1,0:T(8,128)(2,1)} %bitcast.5), custom_call_target="tpu_custom_call" | custom-call | tf_op jit(solution)/shard_map/expand_and_sum/pallas_call | solution.py:510
  59.4 1.7 %divide_bitcast_fusion = f32[1,4,128,128]{3,2,1,0:T(8,128)} fusion(f32[4,128,128]{2,1,0:T(8,128)} %get-tuple-element.7, f32[4,128]{1,0:T(4,128)} %get-tuple-element.8), kind=kLoop, calls=%fused_computation | loop fusion | flops 65536 | bytes 526336 | tf_op jit(solution)/shard_map/broadcast_in_dim | solution.py:562

commit v6 on v5

--- a/solution.py
+++ b/solution.py
@@ -128,7 +128,7 @@
 COPIES = gather_copies()
 N_SMALL = 7 + 3
 N_X = 4 * 6
-N_SUM = 2
+N_SUM = 4
 SEND_SMALL = len(COPIES)
 SEND_SIB = SEND_SMALL + N_SMALL
 SEND_X = SEND_SIB + 4
@@ -145,7 +145,7 @@
     left_set, gather_a, gather_b, stage, products_0, products_1, products_2, products_3, slots_row, slots, meta, meta_s,
     left_s, right_s, out_s, sib_send, sib_recv, partial, half_send, near_send, full_send,
     half_recv, near_recv, full_recv,
-    sums_xy, sums_z, scale, squared, send_sem, recv_sem, local_sem,
+    sums_xy, guests_xy, guest_sum, sums_z, scale, squared, send_sem, recv_sem, local_sem,
 ):
     y, z, layer = lax.axis_index("row"), lax.axis_index("col"), lax.axis_index("layer")
     x, core = layer >> 1, layer & 1
@@ -477,31 +477,72 @@
         d = (4, 3, 5, 2, 6, 1, 7)[n]
         return remote(SEND_SUM + 1, sums_z.at[0], sums_z.at[(-d) % NZ], along_z(d))
 
+    def guest_xy_copy(n):
+        dx, dy = ([(0, 0)] + xy_peers)[n]
+        slot = ((-dx) % NX) * NY + (-dy) % NY
+        target = (ys[dy % NY], z, layers[dx % NX] + 1)
+        return remote(SEND_SUM + 2, sums_xy.at[0], guests_xy.at[slot], target)
+
+    def guest_z_copy(n):
+        d = (4, 3, 5, 2, 6, 1, 7, 0)[n]
+        target = (y, zs[d], layer - 1)
+        return remote(SEND_SUM + 3, guest_sum, sums_z.at[(-d) % NZ], target)
+
+    def drain_x():
+        for jj in range(4):
+            x_copy(jj, 4).wait_send()
+            x_copy(jj, 5).wait_send()
+            stores[jj].wait()
+
+    guest_xy_round = remote(SEND_SUM + 2, guests_xy, guests_xy, sibling)
+    guest_z_round = remote(SEND_SUM + 3, sums_z, sums_z, sibling)
     xy_all = sums_xy.at[pl.ds(1, 15)]
     z_all = sums_z.at[pl.ds(1, 7)]
     xy_round = remote(SEND_SUM, xy_all, xy_all, along_xy(1, 0))
     z_round = remote(SEND_SUM + 1, z_all, z_all, along_z(1))
-    for n in range(15):
-        xy_copy(n).start()
-    total = sums_xy[0]
-    for jj in range(4):
-        x_copy(jj, 4).wait_send()
-        x_copy(jj, 5).wait_send()
-        stores[jj].wait()
-    xy_round.wait_recv()
-    for n in range(1, 16):
-        total = total + sums_xy[n]
-    sums_z[0] = total
-    for n in range(7):
-        z_copy(n).start()
-    xy_round.wait_send()
-    z_round.wait_recv()
+
+    @pl.when(core == 0)
+    def _():
+        for n in (*range(1, 16), 0):
+            guest_xy_copy(n).start()
+        drain_x()
+        guest_xy_round.wait_send()
+        guest_z_round.wait_recv()
+
+    @pl.when(core == 1)
+    def _():
+        for n in range(15):
+            xy_copy(n).start()
+        drain_x()
+        xy_round.wait_recv()
+        total = sums_xy[0]
+        for n in range(1, 16):
+            total = total + sums_xy[n]
+        sums_z[0] = total
+        for n in range(7):
+            z_copy(n).start()
+        guest_xy_round.wait_recv()
+        total = guests_xy[0]
+        for n in range(1, 16):
+            total = total + guests_xy[n]
+        guest_sum[...] = total
+        for n in range(8):
+            guest_z_copy(n).start()
+        xy_round.wait_send()
+        z_round.wait_recv()
+
+    total = sums_z[0]
     for n in range(1, NZ):
         total = total + sums_z[n]
     scale[...] = total / (NY * NZ * 4 * BS) + 1e-6
     last = pltpu.make_async_copy(scale, sums, local_sem.at[13])
     last.start()
-    z_round.wait_send()
+
+    @pl.when(core == 1)
+    def _():
+        z_round.wait_send()
+        guest_z_round.wait_send()
+
     last.wait()
 
 
@@ -541,6 +582,8 @@
             pltpu.VMEM((2, 4, BS // 2, BS), jnp.int16),
             pltpu.VMEM((2, 4, BS // 2 + 16, BS), jnp.int16),
             pltpu.VMEM((16, 4, BS), F32),
+            pltpu.VMEM((16, 4, BS), F32),
+            pltpu.VMEM((4, BS), F32),
             pltpu.VMEM((NZ, 4, BS), F32),
             pltpu.VMEM((4, BS), F32),
             pltpu.VMEM((4, BS, BS), F32),

time: 61.2 us -> 60.7 us (level)
  Pallas kernels: 59.4 us -> 58.6 us
    pallas_call x1, Pallas kernels: 59.4 us -> 58.6 us  [body(): pl.pallas_call(kernel, out_shape=(jax.ShapeDtypeStruct((4, BS, BS), F32),...]
where the time goes in v6:
time: 60.7 us; the launch traced here: 60.3 us
  Pallas kernels  58.6 us (97%)
  other arithmetic  1.68 us (3%)
    pallas_call x1, Pallas kernels, body(): pl.pallas_call(kernel, out_shape=(jax.ShapeDtypeStruct((4, BS, BS), F32),...  58.6 us
    broadcast_in_dim x1, other arithmetic, body(): return (squares / sums[:, None, :])[None]  1.68 us

profile of v6, /device:TPU:2, one launch (start us, length us, event | category | flops | bytes accessed | tf_op | source)
XLA Modules:
  0.0 60.3 jit_solution(2310889709625141270)
XLA Ops:
  0.0 58.6 %expand_and_sum.1 = (f32[4,128,128]{2,1,0:T(8,128)}, f32[4,128]{1,0:T(4,128)}) custom-call(s32[1,64]{1,0:T(1,128)} %left_slots.1, s32[1,4]{1,0:T(1,128)} %right_slots.1, s32[1,32]{1,0:T(1,128)} %out_slots.1, bf16[64,128,128]{2,1,0:T(8,128)(2,1)} %bitcast.4, bf16[512,128]{1,0:T(8,128)(2,1)} %bitcast.5), custom_call_target="tpu_custom_call" | custom-call | tf_op jit(solution)/shard_map/expand_and_sum/pallas_call | solution.py:551
  58.6 1.7 %divide_bitcast_fusion = f32[1,4,128,128]{3,2,1,0:T(8,128)} fusion(f32[4,128,128]{2,1,0:T(8,128)} %get-tuple-element.7, f32[4,128]{1,0:T(4,128)} %get-tuple-element.8), kind=kLoop, calls=%fused_computation | loop fusion | flops 65536 | bytes 526336 | tf_op jit(solution)/shard_map/broadcast_in_dim | solution.py:605
